TPU v7x, 512 devices: a whole 4x8x8 slice. The times are simulated.
512 devices in a mesh: lat: 32 (over y, z_hi), lon: 16 (over x, z_lo, core).
Axes of the slice: x: 4, y: 8, z: 8 (z_hi: 4, z_lo: 2; z = z_hi * 2 + z_lo), core: 2. Of those that a mesh axis runs over, the one named last changes fastest.
Arguments:
- tokens: bfloat16 [128, 512, 384], P('lat', 'lon'), may hold values from -6 to 6
- w_qkv: bfloat16 [384, 1152], replicated, may hold values from -0.3125 to 0.3125
- w_out: bfloat16 [384, 384], replicated, may hold values from -0.3125 to 0.3125
- w_disco: bfloat16 [768, 384], replicated, may hold values from -0.21875 to 0.21875
- psi: float32 [128, 18], P('lat'), may hold values from -2 to 2
- reach: int32 [128], P('lat'), may hold values from 1 to 32, as said below
- key_bias: float32 [128, 8], replicated, may hold values from -4 to 300
- cotangent: bfloat16 [128, 512, 384], P('lat', 'lon'), may hold values from -6 to 6
Outputs:
- mixed_out: bfloat16 [128, 512, 384], P('lat', 'lon')
- input_grad: bfloat16 [128, 512, 384], P('lat', 'lon')
- weight_grads: float32 [884736], P(('lat', 'lon'))
Inputs may be any that keep to these rules, and one draw needn't show every extreme that they name: `reach`: at most 32 in the first and last 8 rows, where some row reaches 32; at most 8 in all other rows, where some row reaches 8.
All inputs are finite; a program needn't handle non-finite values.
Results may differ from a plain program's by a relative error of at most 0.0073.
Values may be sent and summed in bfloat16 or wider, within the bound.
A program may use at most 64 MiB of HBM per device.

v0:
```python
import jax
import jax.numpy as jnp
from jax import lax
from jax.sharding import PartitionSpec as P

HEADS = 8


def extended(block, sides, width, periodic):
    for axis, dim in sides:
        count = lax.axis_size(axis)
        forward = [(i, i + 1) for i in range(count - 1)]
        if periodic:
            forward.append((count - 1, 0))
        backward = [(target, source) for source, target in forward]
        low = lax.ppermute(
            lax.slice_in_dim(block, block.shape[dim] - width, None, axis=dim), axis, forward
        )
        high = lax.ppermute(lax.slice_in_dim(block, 0, width, axis=dim), axis, backward)
        block = jnp.concatenate([low, block, high], axis=dim)
    return block


def product(operand, weight_mat):
    return lax.dot_general(
        operand,
        weight_mat,
        (((operand.ndim - 1,), (0,)), ((), ())),
        preferred_element_type=jnp.float32,
    )


def product_t(operand, weight_mat):
    return lax.dot_general(
        operand,
        weight_mat,
        (((operand.ndim - 1,), (1,)), ((), ())),
        preferred_element_type=jnp.float32,
    )


def cell_sum(former, latter):
    return lax.dot_general(
        former, latter, (((0, 1), (0, 1)), ((), ())), preferred_element_type=jnp.float32
    )


def split_high_low(values):
    high_part = values.astype(jnp.bfloat16)
    low_part = (values - high_part.astype(jnp.float32)).astype(jnp.bfloat16)
    return (high_part, low_part)


def disco_forward(canvas_in, psi_rows):
    row_count = psi_rows.shape[0]
    col_count = canvas_in.shape[1] - 2
    shifted = [
        canvas_in[row_off : row_off + row_count, col_off : col_off + col_count].astype(jnp.float32)
        for row_off in range(3)
        for col_off in range(3)
    ]
    pieces = []
    for basis_idx in range(psi_rows.shape[1] // 9):
        summed = jnp.zeros(shifted[0].shape, jnp.float32)
        for tap_idx in range(9):
            summed = summed + psi_rows[:, basis_idx * 9 + tap_idx][:, None, None] * shifted[tap_idx]
        pieces.append(summed)
    return jnp.concatenate(pieces, axis=-1).astype(jnp.bfloat16)


def disco_backward(grad_s, psi_rows):
    row_count, col_count, all_channels = grad_s.shape
    basis_count = psi_rows.shape[1] // 9
    channels = all_channels // basis_count
    pieces = [
        grad_s[:, :, basis_idx * channels : (basis_idx + 1) * channels].astype(jnp.float32)
        for basis_idx in range(basis_count)
    ]
    canvas = jnp.zeros((row_count + 2, col_count + 2, channels), jnp.float32)
    for row_off in range(3):
        for col_off in range(3):
            tap_idx = row_off * 3 + col_off
            summed = jnp.zeros(pieces[0].shape, jnp.float32)
            for basis_idx in range(basis_count):
                summed = (
                    summed + psi_rows[:, basis_idx * 9 + tap_idx][:, None, None] * pieces[basis_idx]
                )
            canvas = canvas + jnp.pad(
                summed, ((row_off, 2 - row_off), (col_off, 2 - col_off), (0, 0))
            )
    return canvas.astype(jnp.bfloat16)


def attend(queries, kv_frame, bias_rows, reach_rows, row_ok, upstream, key_start, key_span):
    row_count, col_count, channels = queries.shape
    head_dim = channels // HEADS
    scaling = head_dim ** (-0.5)
    key_part = kv_frame[:, key_start : key_start + key_span, :channels].reshape(
        row_count + 2, key_span, HEADS, head_dim
    )
    value_part = kv_frame[:, key_start : key_start + key_span, channels:].reshape(
        row_count + 2, key_span, HEADS, head_dim
    )

    def three_rows(source):
        return jnp.stack([source[row_off : row_off + row_count] for row_off in range(3)], axis=1)

    key_rows = three_rows(key_part)
    value_rows = three_rows(value_part)
    heads_q = queries.reshape(row_count, col_count, HEADS, head_dim)
    heads_up = upstream.reshape(row_count, col_count, HEADS, head_dim)
    bias_three = three_rows(bias_rows).transpose(0, 2, 1)[:, :, None, :, None]
    valid_three = three_rows(row_ok)[:, None, None, :, None]
    offsets = (
        jnp.arange(key_span, dtype=jnp.int32)[None, :]
        + (key_start - col_count)
        - jnp.arange(col_count, dtype=jnp.int32)[:, None]
    )
    in_reach = jnp.abs(offsets)[None] <= reach_rows[:, None, None]
    allowed = in_reach[:, None, :, None, :] & valid_three
    logits = (
        jnp.einsum("rqhd,rakhd->rhqak", heads_q, key_rows, preferred_element_type=jnp.float32)
        * scaling
        + bias_three
    )
    logits = jnp.where(allowed, logits, -jnp.inf)
    attn_probs = jax.nn.softmax(
        logits.reshape(row_count, HEADS, col_count, 3 * key_span), axis=-1
    ).reshape(logits.shape)
    probs_low = attn_probs.astype(jnp.bfloat16)
    attended = (
        jnp.einsum("rhqak,rakhd->rqhd", probs_low, value_rows, preferred_element_type=jnp.float32)
        .astype(jnp.bfloat16)
        .reshape(queries.shape)
    )
    grad_prob = jnp.einsum(
        "rqhd,rakhd->rhqak", heads_up, value_rows, preferred_element_type=jnp.float32
    ).astype(jnp.bfloat16)
    grad_prob = lax.optimization_barrier(grad_prob).astype(jnp.float32)
    grad_logit = attn_probs * (
        grad_prob - jnp.sum(attn_probs * grad_prob, axis=(-2, -1), keepdims=True)
    )
    grad_logit = grad_logit.astype(jnp.bfloat16)
    grad_query = (
        (
            jnp.einsum(
                "rhqak,rakhd->rqhd", grad_logit, key_rows, preferred_element_type=jnp.float32
            )
            * scaling
        )
        .astype(jnp.bfloat16)
        .reshape(queries.shape)
    )
    grad_key = (
        jnp.einsum("rhqak,rqhd->rakhd", grad_logit, heads_q, preferred_element_type=jnp.float32)
        * scaling
    )
    grad_value = jnp.einsum(
        "rhqak,rqhd->rakhd", probs_low, heads_up, preferred_element_type=jnp.float32
    )
    grad_both = jnp.concatenate(
        [
            grad_key.reshape(row_count, 3, key_span, channels),
            grad_value.reshape(row_count, 3, key_span, channels),
        ],
        axis=-1,
    )
    canvas = jnp.zeros((row_count + 2, key_span, 2 * channels), jnp.float32)
    for row_off in range(3):
        canvas = canvas + jnp.pad(grad_both[:, row_off], ((row_off, 2 - row_off), (0, 0), (0, 0)))
    return (attended, grad_query, canvas)


def fold_rims(lon_sum, rim_arrived):
    row_count = lon_sum.shape[0] - 2
    inner_rows = lon_sum[1 : row_count + 1]
    inner_rows = inner_rows.at[0].add(rim_arrived[0])
    return inner_rows.at[row_count - 1].add(rim_arrived[3])


def on_device(tokens, w_qkv, w_out, w_disco, psi, reach, key_bias, cotangent):
    row_count, col_count, channels = tokens.shape
    lat_index = lax.axis_index("lat")
    lat_count = lax.axis_size("lat")
    w_query = w_qkv[:, :channels]
    w_keyval = w_qkv[:, channels:]
    projected = product(tokens, w_qkv).astype(jnp.bfloat16)
    queries = projected[..., :channels]
    payload = jnp.concatenate([tokens, projected[..., channels:]], axis=-1)
    rows_ext = extended(payload, (("lat", 0),), 1, False)
    framed = extended(rows_ext, (("lon", 1),), col_count, True)
    x_frame = framed[..., :channels]
    kv_frame = framed[..., channels:]
    upstream = product_t(cotangent, w_out).astype(jnp.bfloat16)
    padded_bias = jnp.pad(key_bias, ((1, 1), (0, 0)))
    bias_rows = lax.dynamic_slice_in_dim(padded_bias, lat_index * row_count, row_count + 2, 0)
    global_rows = lat_index * row_count - 1 + jnp.arange(row_count + 2, dtype=jnp.int32)
    row_ok = (global_rows >= 0) & (global_rows < lat_count * row_count)
    full_span = 3 * col_count
    attended, grad_query, kv_canvas = attend(
        queries, kv_frame, bias_rows, reach, row_ok, upstream, 0, full_span
    )
    stencil = disco_forward(x_frame[:, col_count - 1 : 2 * col_count + 1], psi)
    mixed_out = (product(attended, w_out) + product(stencil, w_disco)).astype(jnp.bfloat16)
    grad_s = product_t(cotangent, w_disco).astype(jnp.bfloat16)
    disco_canvas = jnp.pad(
        disco_backward(grad_s, psi), ((0, 0), (col_count - 1, col_count - 1), (0, 0))
    )
    kv_part = kv_canvas.astype(jnp.bfloat16)
    returned = jnp.concatenate([kv_part, disco_canvas], axis=-1)
    edge_cols = jnp.concatenate([returned[:, :col_count], returned[:, 2 * col_count :]], axis=1)
    arrived = extended(edge_cols, (("lon", 1),), col_count, True)
    lon_sum = (
        returned[:, col_count : 2 * col_count].astype(jnp.float32)
        + arrived[:, :col_count].astype(jnp.float32)
        + arrived[:, 3 * col_count :].astype(jnp.float32)
    )
    rim_rows = jnp.concatenate([lon_sum[:1], lon_sum[row_count + 1 :]], axis=0)
    rim_arrived = extended(rim_rows.astype(jnp.bfloat16), (("lat", 0),), 1, False).astype(
        rim_rows.dtype
    )
    totals = fold_rims(lon_sum, rim_arrived)
    kv_grad = totals[..., : 2 * channels]
    disco_grad = totals[..., 2 * channels :]
    kv_high, kv_low = split_high_low(kv_grad)
    grads_in = (
        product_t(grad_query, w_query)
        + (product_t(kv_high, w_keyval) + product_t(kv_low, w_keyval))
        + disco_grad
    )
    kv_weight = cell_sum(tokens, kv_high) + cell_sum(tokens, kv_low)
    input_grad = grads_in.astype(jnp.bfloat16)
    query_weight = cell_sum(tokens, grad_query)
    out_weight = cell_sum(attended, cotangent)
    disco_weight = cell_sum(stencil, cotangent)
    flat_grads = jnp.concatenate(
        [
            jnp.concatenate([query_weight, kv_weight], axis=1).reshape(-1),
            out_weight.reshape(-1),
            disco_weight.reshape(-1),
        ]
    )
    weight_grads = lax.psum_scatter(flat_grads, ("lat", "lon"), scatter_dimension=0, tiled=True)
    return (mixed_out, input_grad, weight_grads)


def solution(mesh):
    placed = (
        P("lat", "lon", None),
        P(),
        P(),
        P(),
        P("lat", None),
        P("lat"),
        P(),
        P("lat", "lon", None),
    )
    return jax.shard_map(
        on_device,
        mesh=mesh,
        in_specs=placed,
        out_specs=(P("lat", "lon", None), P("lat", "lon", None), P(("lat", "lon"))),
        check_vma=False,
    )
```

profile of v0, /device:TPU:1, one launch (start us, length us, event | category | flops | bytes accessed | tf_op | source)
XLA Modules:
  0.0 401.6 jit_solution(11549413364712271948)
XLA Ops:
  7.3 1.7 convolution_convert_fusion
  9.0 1.3 collective-permute-start.1
  10.3 7.3 %collective-permute-start = (bf16[1,32,1152]{2,1,0:T(8,128)(2,1)S(1)}, bf16[1,32,1152]{2,1,0:T(8,128)(2,1)S(1)}, u32[]{:S(2)}, u32[]{:S(2)}) collective-permute-start(bf16[1,32,1152]{2,1,0:T(8,128)(2,1)S(1)} %get-tuple-element.60), channel_id=1, source_target_pairs={{0,16},{16,32},{32,48},{48,64},{64,80},{80,96},{96,112},{112,128},... | collective-permute-start | bytes 221192 | tf_op jit(solution)/shard_map/ppermute | solution.py:16
  18.6 0.5 slice_reduce_fusion.17
  19.1 0.3 convolution_convert_fusion.2
  19.7 0.9 reshape.166
  21.1 0.9 add_convert_fusion.1
  22.0 7.0 %collective-permute-start.3 = (bf16[6,32,1152]{2,1,0:T(8,128)(2,1)S(1)}, bf16[6,32,1152]{2,1,0:T(8,128)(2,1)S(1)}, u32[]{:S(2)}, u32[]{:S(2)}) collective-permute-start(bf16[6,32,1152]{2,1,0:T(8,128)(2,1)S(1)} %pad_maximum_fusion.10), channel_id=1, source_target_pairs={{1,0},{2,1},{3,2},{4,3},{5,4},{6,5},{7,6},{8,7},{9,8},{10,9},{11,1... | collective-permute-start | bytes 1327112 | tf_op jit(solution)/shard_map/ppermute | solution.py:19
  29.0 1.9 collective-permute-start.2
  31.1 3.0 collective-permute-done.3
  34.1 5.1 %collective-permute-done.2 = bf16[6,32,1152]{2,1,0:T(8,128)(2,1)S(1)} collective-permute-done((bf16[6,32,1152]{2,1,0:T(8,128)(2,1)S(1)}, bf16[6,32,1152]{2,1,0:T(8,128)(2,1)S(1)}, u32[]{:S(2)}, u32[]{:S(2)}) %collective-permute-start.2) | collective-permute-done | bytes 442400 | tf_op jit(solution)/shard_map/ppermute | solution.py:16
  39.5 0.5 copy-done.5
  39.9 0.9 copy.58
  40.9 0.9 copy.57
  41.8 0.9 copy.56
  43.5 0.7 fusion.83
  44.3 0.5 fusion.5
  44.8 0.4 copy-done.24
  45.5 0.7 fusion.18
  46.4 0.4 convolution_convert_fusion.1
  46.8 2.1 convolution_bitcast_fusion
  48.9 0.6 fusion.1
  49.5 0.5 fusion.3
  50.1 0.4 copy-done.11
  50.5 0.5 multiply_bitcast_fusion
  51.0 0.5 copy-done.19
  51.7 1.2 fusion.17
  53.0 0.8 copy.74
  53.8 1.2 reshape.165
  55.0 1.6 copy.78
  56.6 2.9 copy.81
  59.5 1.9 copy.80
  61.4 1.8 copy.82
  63.2 2.2 fusion.15
  65.7 0.7 copy-done.12
  66.5 1.0 fusion.79
  67.5 3.5 collective-permute-start.5
  71.0 3.0 collective-permute-start.4
  74.0 0.8 copy.76
  74.8 1.8 reshape.167
  76.7 0.3 fusion.58
  77.0 0.3 fusion.49
  77.4 0.3 copy-done.30
  77.7 0.6 copy-done.32
  78.3 0.3 convolution_bitcast_fusion.1
  78.7 1.1 reshape.172
  80.0 0.9 reshape.171
  80.9 0.6 collective-permute-done.5
  81.4 1.2 collective-permute-done.4
  82.7 1.3 fusion.78
  84.0 1.3 collective-permute-start.7
  85.3 7.5 %collective-permute-start.6 = (bf16[1,32,1152]{2,1,0:T(8,128)(2,1)S(1)}, bf16[1,32,1152]{2,1,0:T(8,128)(2,1)S(1)}, u32[]{:S(2)}, u32[]{:S(2)}) collective-permute-start(bf16[1,32,1152]{2,1,0:T(8,128)(2,1)S(1)} %get-tuple-element.58), channel_id=1, source_target_pairs={{0,16},{16,32},{32,48},{48,64},{64,80},{80,96},{96,112},{112,128},... | collective-permute-start | bytes 221192 | tf_op jit(solution)/shard_map/ppermute | solution.py:16
  93.2 1.1 collective-permute-done.6
  94.3 0.3 convolution_bitcast_fusion.2
  94.6 0.3 fusion.7
  95.1 1.9 copy.83
  97.0 1.6 reshape.170
  98.6 3.3 pad_maximum_fusion
  101.9 0.9 copy-done.9
  103.1 0.9 fusion.20
  104.3 0.3 convolution_add_fusion
  104.7 0.9 fusion.21
  105.6 287.8 %all-reduce.17.cloned.1.call-done = f32[884736]{0:T(1024)} async-done(((f32[884736]{0:T(1024)}), f32[884736]{0:T(1024)}) %all-reduce.17.cloned.1.call-update) | async-done | bytes 3538960
  393.4 1.4 dynamic-slice.14
  (121 shorter events, 5.4 us)
Async XLA Ops:
  7.2 11.9 %copy-start = (bf16[768,384]{1,0:T(8,128)(2,1)S(1)}, bf16[768,384]{1,0:T(8,128)(2,1)}, u32[]{:S(2)}) copy-start(bf16[768,384]{1,0:T(8,128)(2,1)} %param.15) | copy-start | bytes 1769476
  7.2 1.8 copy-start.2
  7.2 10.4 %copy-start.40 = (f32[128,8]{0,1:T(8,128)S(1)}, f32[128,8]{0,1:T(8,128)}, u32[]{:S(2)}) copy-start(f32[128,8]{0,1:T(8,128)} %param.18) | copy-start | bytes 12292
  7.2 11.4 %copy-start.13 = (f32[4,18]{1,0:T(4,128)S(1)}, f32[4,18]{1,0:T(4,128)}, u32[]{:S(2)}) copy-start(f32[4,18]{1,0:T(4,128)} %param.16) | copy-start | bytes 868
  7.2 11.9 %copy-start.27 = (bf16[4,32,384]{2,1,0:T(8,128)(2,1)S(1)}, bf16[4,32,384]{2,1,0:T(8,128)(2,1)}, u32[]{:S(2)}) copy-start(bf16[4,32,384]{2,1,0:T(8,128)(2,1)} %param.19) | copy-start | bytes 294916
  7.2 12.2 %copy-start.8 = (bf16[384,384]{1,0:T(8,128)(2,1)S(1)}, bf16[384,384]{1,0:T(8,128)(2,1)}, u32[]{:S(2)}) copy-start(bf16[384,384]{1,0:T(8,128)(2,1)} %param.14) | copy-start | bytes 884740
  7.2 386.1 %all-reduce.17.cloned.1.call-start = ((), (), s32[]{:S(2)}) async-start(), calls=%async_computation | async-start | bytes 7077888
  9.0 13.0 %collective-permute-start.1 = (bf16[1,32,1152]{2,1,0:T(8,128)(2,1)S(1)}, bf16[1,32,1152]{2,1,0:T(8,128)(2,1)S(1)}, u32[]{:S(2)}, u32[]{:S(2)}) collective-permute-start(bf16[1,32,1152]{2,1,0:T(8,128)(2,1)S(1)} %get-tuple-element.61), channel_id=1, source_target_pairs={{16,0},{32,16},{48,32},{64,48},{80,64},{96,80},{112,96},{128,112},... | collective-permute-start | bytes 221192 | tf_op jit(solution)/shard_map/ppermute | solution.py:19
  10.3 11.7 %collective-permute-start = (bf16[1,32,1152]{2,1,0:T(8,128)(2,1)S(1)}, bf16[1,32,1152]{2,1,0:T(8,128)(2,1)S(1)}, u32[]{:S(2)}, u32[]{:S(2)}) collective-permute-start(bf16[1,32,1152]{2,1,0:T(8,128)(2,1)S(1)} %get-tuple-element.60), channel_id=1, source_target_pairs={{0,16},{16,32},{32,48},{48,64},{64,80},{80,96},{96,112},{112,128},... | collective-permute-start | bytes 221192 | tf_op jit(solution)/shard_map/ppermute | solution.py:16
  18.4 25.1 %copy-start.10 = (bf16[4,32,8,48]{3,2,1,0:T(8,128)(2,1)}, bf16[4,32,8,48]{3,2,1,0:T(8,128)(2,1)S(1)}, u32[]{:S(2)}) copy-start(bf16[4,32,8,48]{3,2,1,0:T(8,128)(2,1)S(1)} %reshape.164) | copy-start | bytes 294916
  19.1 1.8 copy-start.36
  19.1 1.8 copy-start.38
  21.1 9.8 %copy-start.41 = (s32[4]{0:T(128)S(1)}, s32[4]{0:T(128)}, u32[]{:S(2)}) copy-start(s32[4]{0:T(128)} %param.17) | copy-start | bytes 52
  22.0 12.1 %collective-permute-start.3 = (bf16[6,32,1152]{2,1,0:T(8,128)(2,1)S(1)}, bf16[6,32,1152]{2,1,0:T(8,128)(2,1)S(1)}, u32[]{:S(2)}, u32[]{:S(2)}) collective-permute-start(bf16[6,32,1152]{2,1,0:T(8,128)(2,1)S(1)} %pad_maximum_fusion.10), channel_id=1, source_target_pairs={{1,0},{2,1},{3,2},{4,3},{5,4},{6,5},{7,6},{8,7},{9,8},{10,9},{11,1... | collective-permute-start | bytes 1327112 | tf_op jit(solution)/shard_map/ppermute | solution.py:19
  29.0 10.2 %collective-permute-start.2 = (bf16[6,32,1152]{2,1,0:T(8,128)(2,1)S(1)}, bf16[6,32,1152]{2,1,0:T(8,128)(2,1)S(1)}, u32[]{:S(2)}, u32[]{:S(2)}) collective-permute-start(bf16[6,32,1152]{2,1,0:T(8,128)(2,1)S(1)} %pad_maximum_fusion.10), channel_id=1, source_target_pairs={{0,1},{1,2},{2,3},{3,4},{4,5},{5,6},{6,7},{7,8},{8,9},{9,10},{10,1... | collective-permute-start | bytes 1327112 | tf_op jit(solution)/shard_map/ppermute | solution.py:16
  34.1 5.4 %copy-start.3 = (bf16[6,32,1152]{2,1,0:T(8,128)(2,1)}, bf16[6,32,1152]{2,1,0:T(8,128)(2,1)S(1)}, u32[]{:S(2)}) copy-start(bf16[6,32,1152]{2,1,0:T(8,128)(2,1)S(1)} %collective-permute-done.3) | copy-start | bytes 1327108
  39.1 0.8 copy-start.5
  42.9 1.3 copy-start.18
  43.2 1.0 copy-start.20
  43.4 0.8 copy-start.22
  44.2 1.0 copy-start.24
  44.2 1.1 copy-start.25
  44.2 1.2 copy-start.26
  45.5 0.9 copy-start.34
  49.5 1.0 copy-start.11
  50.5 1.0 copy-start.19
  50.5 1.1 copy-start.21
  50.5 1.2 copy-start.23
  55.0 24.8 %copy-start.14 = (bf16[4,32,384]{2,1,0:T(8,128)(2,1)}, bf16[4,32,384]{2,1,0:T(8,128)(2,1)S(1)}, u32[]{:S(2)}) copy-start(bf16[4,32,384]{2,1,0:T(8,128)(2,1)S(1)} %reshape.165) | copy-start | bytes 294916
  65.5 0.9 copy-start.12
  66.4 7.7 %copy-start.35 = (bf16[4,32,8,48]{3,1,2,0:T(8,128)(2,1)S(1)}, bf16[4,32,8,48]{3,1,2,0:T(8,128)(2,1)}, u32[]{:S(2)}) copy-start(bf16[4,32,8,48]{3,1,2,0:T(8,128)(2,1)} %fusion.17) | copy-start | bytes 294916
  66.5 10.2 %copy-start.4 = (bf16[6,32,1152]{2,1,0:T(8,128)(2,1)S(1)}, bf16[6,32,1152]{2,1,0:T(8,128)(2,1)}, u32[]{:S(2)}) copy-start(bf16[6,32,1152]{2,1,0:T(8,128)(2,1)} %copy-done.3) | copy-start | bytes 1327108
  66.5 10.2 %copy-start.6 = (bf16[6,32,1152]{2,1,0:T(8,128)(2,1)S(1)}, bf16[6,32,1152]{2,1,0:T(8,128)(2,1)}, u32[]{:S(2)}) copy-start(bf16[6,32,1152]{2,1,0:T(8,128)(2,1)} %copy-done.5) | copy-start | bytes 1327108
  66.5 10.2 %copy-start.37 = (f32[4]{0:T(128)S(1)}, f32[4]{0:T(128)}, u32[]{:S(2)}) copy-start(f32[4]{0:T(128)} %copy-done.36) | copy-start | bytes 52
  66.5 10.2 %copy-start.39 = (f32[4]{0:T(128)S(1)}, f32[4]{0:T(128)}, u32[]{:S(2)}) copy-start(f32[4]{0:T(128)} %copy-done.38) | copy-start | bytes 52
  67.5 13.9 %collective-permute-start.5 = (bf16[6,32,1152]{2,1,0:T(8,128)(2,1)}, bf16[6,32,1152]{2,1,0:T(8,128)(2,1)}, u32[]{:S(2)}, u32[]{:S(2)}) collective-permute-start(bf16[6,32,1152]{2,1,0:T(8,128)(2,1)} %get-tuple-element.51), channel_id=1, source_target_pairs={{1,0},{2,1},{3,2},{4,3},{5,4},{6,5},{7,6},{8,7},{9,8},{10,9},{11,1... | collective-permute-start | bytes 1327112 | tf_op jit(solution)/shard_map/ppermute | solution.py:19
  71.0 11.7 %collective-permute-start.4 = (bf16[6,32,1152]{2,1,0:T(8,128)(2,1)}, bf16[6,32,1152]{2,1,0:T(8,128)(2,1)}, u32[]{:S(2)}, u32[]{:S(2)}) collective-permute-start(bf16[6,32,1152]{2,1,0:T(8,128)(2,1)} %get-tuple-element.50), channel_id=1, source_target_pairs={{0,1},{1,2},{2,3},{3,4},{4,5},{5,6},{6,7},{7,8},{8,9},{9,10},{10,1... | collective-permute-start | bytes 1327112 | tf_op jit(solution)/shard_map/ppermute | solution.py:16
  76.7 1.6 copy-start.28
  77.0 0.6 copy-start.30
  77.7 0.6 copy-start.32
  78.6 1.1 copy-start.29
  80.9 12.0 %copy-start.16 = (bf16[4,32,384]{2,1,0:T(8,128)(2,1)S(1)}, bf16[4,32,384]{2,1,0:T(8,128)(2,1)}, u32[]{:S(2)}) copy-start(bf16[4,32,384]{2,1,0:T(8,128)(2,1)} %reshape.167) | copy-start | bytes 294916
  84.0 9.2 %collective-permute-start.7 = (bf16[1,32,1152]{2,1,0:T(8,128)(2,1)S(1)}, bf16[1,32,1152]{2,1,0:T(8,128)(2,1)S(1)}, u32[]{:S(2)}, u32[]{:S(2)}) collective-permute-start(bf16[1,32,1152]{2,1,0:T(8,128)(2,1)S(1)} %get-tuple-element.59), channel_id=1, source_target_pairs={{16,0},{32,16},{48,32},{64,48},{80,64},{96,80},{112,96},{128,112},... | collective-permute-start | bytes 221192 | tf_op jit(solution)/shard_map/ppermute | solution.py:19
  85.3 8.9 %collective-permute-start.6 = (bf16[1,32,1152]{2,1,0:T(8,128)(2,1)S(1)}, bf16[1,32,1152]{2,1,0:T(8,128)(2,1)S(1)}, u32[]{:S(2)}, u32[]{:S(2)}) collective-permute-start(bf16[1,32,1152]{2,1,0:T(8,128)(2,1)S(1)} %get-tuple-element.58), channel_id=1, source_target_pairs={{0,16},{16,32},{32,48},{48,64},{64,80},{80,96},{96,112},{112,128},... | collective-permute-start | bytes 221192 | tf_op jit(solution)/shard_map/ppermute | solution.py:16
  97.0 1.6 copy-start.7
  101.9 1.0 copy-start.9
  101.9 1.0 copy-start.15
  101.9 1.2 copy-start.31
  101.9 1.2 copy-start.33
  101.9 2.1 copy-start.1
  103.1 1.6 copy-start.17
Sparse Core Ops, SparseCore 0:
  102.1 291.2 all-reduce.16
where the time goes:
time: 403 us; the launch traced here: 402 us
  waiting for transfers between devices  299 us (74%)
  starting transfers between devices  32.8 us (8%)
  local copies, waits for them, and re-layouts  32.1 us (8%)
  between operations  14.8 us (4%)
  matrix products  12 us (3%)
  other arithmetic  11.2 us (3%)
    unnamed x2, waiting for transfers between devices  288 us
    ppermute x4, starting transfers between devices, extended(): lax.ppermute(lax.slice_in_dim(block, block.shape[dim] - width, None, axis...  19.7 us
    ppermute x4, starting transfers between devices, extended(): lax.ppermute(lax.slice_in_dim(block, 0, width, axis=dim), axis, backward)  13 us
  transfers between devices with their start and end apart: 9, of which 6 were waited for; matrix products, arithmetic and copies ran while one was open for 3% of the time, Pallas kernels for 0%

commit v1 on v0

v1 whole, which is shorter than its diff:
```python
import jax
import jax.numpy as jnp
from jax import lax
from jax.experimental import pallas as pl
from jax.experimental.pallas import tpu as pltpu
from jax.sharding import PartitionSpec as P

HEADS = 8
HEAD_DIM = 48
C = 384
ROWS = 4
COLS = 32
SPAN = 3 * COLS
FRAME = (ROWS + 2) * SPAN
CELLS = ROWS * COLS
LATS = 32
LONS = 16
CHUNK = 144
SCALING = HEAD_DIM ** (-0.5)
FAR = -1e30
MESH = pl.DeviceIdType.MESH
BF16 = jnp.bfloat16
F32 = jnp.float32
VMEM = pltpu.VMEM
LIMIT = 56 * 1024 * 1024


def nn(left, right):
    return lax.dot_general(left, right, (((1,), (0,)), ((), ())), preferred_element_type=F32)


def nt(left, right):
    return lax.dot_general(left, right, (((1,), (1,)), ((), ())), preferred_element_type=F32)


def tn(left, right):
    return lax.dot_general(left, right, (((0,), (0,)), ((), ())), preferred_element_type=F32)


def place():
    return lax.axis_index("lat"), lax.axis_index("lon")


def neighbours(lat, lon):
    found = []
    for row_step in (-1, 0, 1):
        for col_step in (-1, 0, 1):
            if row_step or col_step:
                target = (
                    lax.rem(lat + row_step + LATS, LATS),
                    lax.rem(lon + col_step + LONS, LONS),
                )
                found.append((row_step, col_step, target))
    return found


def greet(targets, count):
    barrier = pltpu.get_barrier_semaphore()
    for target in targets:
        pl.semaphore_signal(barrier, inc=1, device_id=target, device_id_type=MESH)
    pl.semaphore_wait(barrier, count)


def halo_kernel(tokens_ref, frame_ref, send_sem, recv_sem):
    lat, lon = place()
    around = neighbours(lat, lon)
    greet([target for _, _, target in around], len(around))
    copies = []
    for idx, (row_step, col_step, target) in enumerate(around):
        if row_step == -1:
            src, dst_rows = tokens_ref.at[pl.ds(0, 1)], pl.ds(ROWS + 1, 1)
        elif row_step == 1:
            src, dst_rows = tokens_ref.at[pl.ds(ROWS - 1, 1)], pl.ds(0, 1)
        else:
            src, dst_rows = tokens_ref, pl.ds(1, ROWS)
        copy = pltpu.make_async_remote_copy(
            src_ref=src,
            dst_ref=frame_ref.at[dst_rows, pl.ds((1 - col_step) * COLS, COLS)],
            send_sem=send_sem.at[idx],
            recv_sem=recv_sem.at[idx],
            device_id=target,
            device_id_type=MESH,
        )
        copy.start()
        copies.append(copy)
    frame_ref[1 : ROWS + 1, COLS : 2 * COLS] = tokens_ref[...]
    for copy in copies:
        copy.wait()

    @pl.when(lat == 0)
    def _():
        frame_ref[0] = jnp.zeros((SPAN, C), BF16)

    @pl.when(lat == LATS - 1)
    def _():
        frame_ref[ROWS + 1] = jnp.zeros((SPAN, C), BF16)


def halo(tokens):
    return pl.pallas_call(
        halo_kernel,
        out_shape=jax.ShapeDtypeStruct((ROWS + 2, SPAN, C), BF16),
        in_specs=[pl.BlockSpec(memory_space=VMEM)],
        out_specs=pl.BlockSpec(memory_space=VMEM),
        scratch_shapes=[pltpu.SemaphoreType.DMA((8,)), pltpu.SemaphoreType.DMA((8,))],
        compiler_params=pltpu.CompilerParams(
            collective_id=0, has_side_effects=True, vmem_limit_bytes=LIMIT
        ),
    )(tokens)


def block_kernel(
    frame_ref,
    cot_ref,
    w_qkv_ref,
    w_out_ref,
    w_disco_ref,
    psi_ref,
    reach_ref,
    bias_ref,
    mixed_ref,
    own_ref,
    rim_ref,
    grads_ref,
    kv_ref,
    canvas_ref,
    shifted_ref,
    stencil_ref,
    att_ref,
    dq_ref,
    gs_ref,
):
    lat, _ = place()
    x_own = jnp.concatenate(
        [frame_ref[(r + 1) * SPAN + COLS : (r + 1) * SPAN + 2 * COLS] for r in range(ROWS)], axis=0
    )
    cot = cot_ref[...].reshape(CELLS, C)
    queries = nn(x_own, w_qkv_ref[:, :C]).astype(BF16)
    upstream = nt(cot, w_out_ref[...]).astype(BF16)
    gs_ref[...] = nt(cot, w_disco_ref[...]).astype(BF16).astype(F32)
    for r in range(ROWS + 2):
        rows = slice(r * SPAN, (r + 1) * SPAN)
        kv_ref[rows] = nn(frame_ref[rows], w_qkv_ref[:, C:]).astype(BF16)
    canvas_ref[...] = jnp.zeros_like(canvas_ref)

    for r in range(ROWS + 2):
        wide = frame_ref[r * SPAN + 16 : r * SPAN + 80].astype(F32)
        shifted_ref[0, r] = pltpu.roll(wide, 1, 0)[16:48]
        shifted_ref[1, r] = wide[16:48]
        shifted_ref[2, r] = pltpu.roll(wide, 63, 0)[16:48]
    for r in range(ROWS):
        for k in range(2):
            total = jnp.zeros((COLS, C), F32)
            for a in range(3):
                for b in range(3):
                    total = total + psi_ref[r, 9 * k + 3 * a + b] * shifted_ref[b, r + a]
            stencil_ref[r * COLS : (r + 1) * COLS, k * C : (k + 1) * C] = total.astype(BF16)

    stack = HEADS * COLS
    head_mask = (
        lax.broadcasted_iota(jnp.int32, (stack, C), 0) // COLS
        == lax.broadcasted_iota(jnp.int32, (stack, C), 1) // HEAD_DIM
    )
    head_mask = jnp.where(head_mask, 1.0, 0.0).astype(BF16)
    lane_head = lax.broadcasted_iota(jnp.int32, (COLS, C), 1) // HEAD_DIM
    distance = jnp.abs(
        lax.broadcasted_iota(jnp.int32, (SPAN, stack), 0)
        - COLS
        - lax.rem(lax.broadcasted_iota(jnp.int32, (SPAN, stack), 1), COLS)
    )
    stack_head = lax.broadcasted_iota(jnp.int32, (1, stack), 1) // COLS
    bias_rows = []
    for k in range(ROWS + 2):
        global_row = lat * ROWS - 1 + k
        clamped = jnp.clip(global_row, 0, LATS * ROWS - 1)
        line = jnp.zeros((1, stack), F32)
        for h in range(HEADS):
            line = jnp.where(stack_head == h, bias_ref[clamped, h], line)
        valid = (global_row >= 0) & (global_row < LATS * ROWS)
        bias_rows.append(jnp.where(valid, line, FAR))

    def fold_heads(wide):
        total = jnp.zeros((COLS, C), F32)
        for h in range(HEADS):
            total = jnp.where(lane_head == h, wide[h * COLS : (h + 1) * COLS], total)
        return total

    for r in range(ROWS):
        cells = slice(r * COLS, (r + 1) * COLS)
        keys_at = slice(r * SPAN, (r + 3) * SPAN)
        keys, values = kv_ref[keys_at, :C], kv_ref[keys_at, C:]
        q_heads = jnp.concatenate([queries[cells]] * HEADS, axis=0) * head_mask
        u_heads = jnp.concatenate([upstream[cells]] * HEADS, axis=0) * head_mask
        outside = jnp.where(distance <= reach_ref[r], 0.0, FAR)
        added = jnp.concatenate([outside + bias_rows[r + a] for a in range(3)], axis=0)
        logits = nt(keys, q_heads) * SCALING + added
        logits = logits - jnp.max(logits, axis=0, keepdims=True)
        probs = jnp.exp(logits)
        probs = probs * (1.0 / jnp.sum(probs, axis=0, keepdims=True))
        probs_low = probs.astype(BF16)
        grad_prob = nt(values, u_heads).astype(BF16).astype(F32)
        mean = jnp.sum(probs * grad_prob, axis=0, keepdims=True)
        grad_logit = (probs * (grad_prob - mean)).astype(BF16)
        att_ref[cells] = fold_heads(tn(probs_low, values)).astype(BF16)
        dq_ref[cells] = (fold_heads(tn(grad_logit, keys)) * SCALING).astype(BF16)
        canvas_ref[keys_at, :C] += nn(grad_logit, q_heads) * SCALING
        canvas_ref[keys_at, C:] += nn(probs_low, u_heads)

    attended = att_ref[...]
    grad_query = dq_ref[...]
    stencil = stencil_ref[...]
    mixed = nn(attended, w_out_ref[...]) + nn(stencil, w_disco_ref[...])
    mixed_ref[...] = mixed.astype(BF16).reshape(ROWS, COLS, C)
    grads_ref[1, :C] = tn(attended, cot).astype(BF16)
    grads_ref[1, C:] = tn(stencil, cot).astype(BF16)

    kv_part = canvas_ref[...].astype(BF16)
    query_weight = tn(x_own, grad_query).astype(BF16)
    kv_weight = tn(frame_ref[...], kv_part).astype(BF16)
    for c in range(8):
        lines = slice(48 * c, 48 * (c + 1))
        grads_ref[0, CHUNK * c : CHUNK * c + 48] = query_weight[lines]
        grads_ref[0, CHUNK * c + 48 : CHUNK * c + 96] = kv_weight[lines, :C]
        grads_ref[0, CHUNK * c + 96 : CHUNK * c + 144] = kv_weight[lines, C:]

    canvas_ref[:, :C] = nt(kv_part, w_qkv_ref[:, C:])
    query_part = nt(grad_query, w_qkv_ref[:, :C])
    margin = jnp.zeros((16, C), F32)
    for row in range(ROWS + 2):
        spread = jnp.zeros((64, C), F32)
        for b in range(3):
            total = jnp.zeros((COLS, C), F32)
            for a in range(3):
                r = row - a
                if 0 <= r < ROWS:
                    for k in range(2):
                        total = total + (
                            psi_ref[r, 9 * k + 3 * a + b]
                            * gs_ref[r * COLS : (r + 1) * COLS, k * C : (k + 1) * C]
                        )
            total = jnp.concatenate([margin, total, margin], axis=0)
            spread = spread + (total if b == 1 else pltpu.roll(total, 63 if b == 0 else 1, 0))
        canvas_ref[row * SPAN + 16 : row * SPAN + 80, :C] += spread
    for r in range(ROWS):
        at = (r + 1) * SPAN + COLS
        own_ref[r] = canvas_ref[at : at + COLS, :C] + query_part[r * COLS : (r + 1) * COLS]
    rim_ref[...] = canvas_ref[:, :C].astype(BF16).reshape(ROWS + 2, SPAN, C)


def block(frame, cotangent, w_qkv, w_out, w_disco, psi, reach, key_bias):
    vmem = pl.BlockSpec(memory_space=VMEM)
    smem = pl.BlockSpec(memory_space=pltpu.SMEM)
    return pl.pallas_call(
        block_kernel,
        out_shape=(
            jax.ShapeDtypeStruct((ROWS, COLS, C), BF16),
            jax.ShapeDtypeStruct((ROWS, COLS, C), F32),
            jax.ShapeDtypeStruct((ROWS + 2, SPAN, C), BF16),
            jax.ShapeDtypeStruct((2, 8 * CHUNK, C), BF16),
        ),
        in_specs=[vmem] * 5 + [smem] * 3,
        out_specs=(vmem,) * 4,
        scratch_shapes=[
            VMEM((FRAME, 2 * C), BF16),
            VMEM((FRAME, 2 * C), F32),
            VMEM((3, ROWS + 2, COLS, C), F32),
            VMEM((CELLS, 2 * C), BF16),
            VMEM((CELLS, C), BF16),
            VMEM((CELLS, C), BF16),
            VMEM((CELLS, 2 * C), F32),
        ],
        compiler_params=pltpu.CompilerParams(vmem_limit_bytes=LIMIT),
    )(frame, cotangent, w_qkv, w_out, w_disco, psi, reach, key_bias)


def sum_kernel(
    grads_ref,
    own_ref,
    rim_ref,
    input_ref,
    weight_ref,
    pair_in,
    x_out,
    x_in,
    total_ref,
    z_out,
    z_in,
    last_out,
    last_in,
    rim_in,
    line_in,
    order_ref,
    pair_send,
    pair_recv,
    x_send,
    x_recv,
    z_send,
    z_recv,
    last_send,
    last_recv,
    rim_send,
    rim_recv,
):
    lat, lon = place()
    y, z_high = lat // 4, lax.rem(lat, 4)
    x, z_low, core = lon // 4, lax.rem(lon, 4) // 2, lax.rem(lon, 2)
    z = z_high * 2 + z_low
    other = 1 - core
    pair_peer = (lat, lon + 1 - 2 * core)
    x_peers = []
    for d in range(1, 4):
        peer_x = lax.rem(x + d, 4)
        peer_back = lax.rem(x + 4 - d, 4)
        x_peers.append((peer_x, (lat, peer_x * 4 + lax.rem(lon, 4)), (lat, peer_back * 4 + lax.rem(lon, 4))))

    def at_z(where):
        return (y * 4 + where // 2, x * 4 + lax.rem(where, 2) * 2 + core)

    z_peers = []
    for d in range(1, 8):
        peer_z, back = lax.rem(z + d, 8), lax.rem(z + 8 - d, 8)
        z_peers.append((peer_z, at_z(peer_z), at_z(back)))
    around = neighbours(lat, lon)
    owners = []
    for job in range(2):
        for o in range(4):
            owners.append((job * 16 + 2 * (core * 4 + x) + z // 4, 4 * lax.rem(z, 4) + o))
    piece = lax.rem(lat, 16) * 16 + lon
    chunk = piece // 32
    from_x, from_core = lax.rem(chunk, 4), chunk // 4
    from_z = lax.rem(piece, 32) // 4
    sources = []
    for k in range(8):
        sources.append((k * 4 + from_z // 2, from_x * 4 + lax.rem(from_z, 2) * 2 + from_core))

    barrier = pltpu.get_barrier_semaphore()

    def hail(target):
        pl.semaphore_signal(barrier, inc=1, device_id=target, device_id_type=MESH)

    hail(pair_peer)
    for _, _, back in x_peers:
        hail(back)
    for _, _, back in z_peers:
        hail(back)
    for _, _, target in around:
        hail(target)
    expected = 1 + 3 + 7 + 8 + 8
    for source in sources:
        same = (source[0] == lat) & (source[1] == lon)

        @pl.when(jnp.logical_not(same))
        def _():
            hail(source)

    for owner in owners:
        same = (owner[0] == lat) & (owner[1] == lon)
        expected = expected - jnp.where(same, 1, 0)
    pl.semaphore_wait(barrier, expected)

    def remote(src, dst, send, recv, target):
        return pltpu.make_async_remote_copy(
            src_ref=src,
            dst_ref=dst,
            send_sem=send,
            recv_sem=recv,
            device_id=target,
            device_id_type=MESH,
        )

    jobs = (1, 0)
    pending = []
    pair_copies = {}
    for job in jobs:
        copy = remote(
            grads_ref.at[job, pl.ds(other * 4, 4)],
            pair_in.at[job],
            pair_send.at[job],
            pair_recv.at[job],
            pair_peer,
        )
        copy.start()
        pair_copies[job] = copy
    rim_copies = []
    for idx, (row_step, col_step, target) in enumerate(around):
        if row_step == 0:
            src = rim_ref.at[pl.ds(1, ROWS), pl.ds((1 + col_step) * COLS, COLS)]
            dst = rim_in.at[0 if col_step == -1 else 1]
        else:
            row = 0 if row_step == -1 else ROWS + 1
            src = rim_ref.at[row, pl.ds((1 + col_step) * COLS, COLS)]
            dst = line_in.at[(0 if row_step == -1 else 3) + col_step + 1]
        copy = remote(src, dst, rim_send.at[idx], rim_recv.at[idx], target)
        copy.start()
        rim_copies.append(copy)

    x_copies = {}
    for job in jobs:
        pair_copies[job].wait()
        x_copies[job] = []
        for d, (peer_x, target, _) in enumerate(x_peers):
            added = grads_ref[job, core * 4 + peer_x].astype(F32) + pair_in[job, peer_x].astype(F32)
            x_out[job, d] = added.astype(BF16)
            copy = remote(
                x_out.at[job, d], x_in.at[job, d], x_send.at[job, d], x_recv.at[job, d], target
            )
            copy.start()
            x_copies[job].append(copy)

    row_ids = lax.broadcasted_iota(jnp.int32, (16, C), 0)
    z_copies = {}
    for job in jobs:
        total = grads_ref[job, core * 4 + x].astype(F32) + pair_in[job, x].astype(F32)
        for d in range(3):
            x_copies[job][d].wait()
            total = total + x_in[job, d].astype(F32)
        total_ref[job, 0:8] = jnp.zeros((8, C), F32)
        total_ref[job, 8 : 8 + CHUNK] = total
        total_ref[job, 8 + CHUNK : 32 + CHUNK] = jnp.zeros((24, C), F32)
        for k in range(8):
            for half in range(2):
                if job == 1:
                    first = 8 + 18 * k + 9 * half
                    lines = total_ref[job, first : first + 16]
                else:
                    first = 8 + 6 * k + 3 * half
                    parts = [
                        total_ref[job, first + 48 * m - 3 * m : first + 48 * m - 3 * m + 16]
                        for m in range(3)
                    ]
                    lines = jnp.where(row_ids < 3, parts[0], jnp.where(row_ids < 6, parts[1], parts[2]))
                z_out[job, k, half * 16 : half * 16 + 16] = lines.astype(BF16)
        z_copies[job] = []
        for d, (peer_z, target, _) in enumerate(z_peers):
            copy = remote(
                z_out.at[job, peer_z], z_in.at[job, d], z_send.at[job, d], z_recv.at[job, d], target
            )
            copy.start()
            z_copies[job].append(copy)

    for idx, copy in enumerate(rim_copies):
        copy.wait()
    above = jnp.where(lat > 0, 1.0, 0.0)
    below = jnp.where(lat < LATS - 1, 1.0, 0.0)
    for r in range(ROWS):
        summed = own_ref[r] + rim_in[0, r].astype(F32) + rim_in[1, r].astype(F32)
        for side in range(3):
            if r == 0:
                summed = summed + above * line_in[3 + side].astype(F32)
            if r == ROWS - 1:
                summed = summed + below * line_in[side].astype(F32)
        input_ref[r] = summed.astype(BF16)

    for job in jobs:
        total = z_out[job, z].astype(F32)
        for d in range(7):
            z_copies[job][d].wait()
            total = total + z_in[job, d].astype(F32)
        last_out[job] = total.astype(BF16)
        for o in range(4):
            owner = owners[job * 4 + o]
            same = (owner[0] == lat) & (owner[1] == lon)
            src = last_out.at[job, pl.ds((o // 2) * 16, 16)]

            @pl.when(jnp.logical_not(same))
            def _():
                remote(src, last_in.at[y], last_send.at[job, o], last_recv.at[y], owner).start()

            @pl.when(same)
            def _():
                last_in[y] = src[...]

    final = jnp.zeros((16, C), F32)
    for k in range(8):
        same = (sources[k][0] == lat) & (sources[k][1] == lon)

        @pl.when(jnp.logical_not(same))
        def _():
            remote(
                last_out.at[0, pl.ds(0, 16)],
                last_in.at[k],
                last_send.at[0, 0],
                last_recv.at[k],
                sources[k],
            ).wait_recv()

        final = final + last_in[k].astype(F32)
    for job in jobs:
        for o in range(4):
            owner = owners[job * 4 + o]
            same = (owner[0] == lat) & (owner[1] == lon)

            @pl.when(jnp.logical_not(same))
            def _():
                remote(
                    last_out.at[job, pl.ds((o // 2) * 16, 16)],
                    last_in.at[y],
                    last_send.at[job, o],
                    last_recv.at[y],
                    owner,
                ).wait_send()

    order_ref[0:16] = jnp.zeros((16, C), F32)
    order_ref[16:32] = final
    order_ref[32:48] = jnp.zeros((16, C), F32)
    mixed = final
    for i in range(3):
        for m in range(3):
            target, origin = 3 * i + m, 3 * m + i
            first = 16 + origin - target
            mixed = jnp.where(row_ids == target, order_ref[first : first + 16], mixed)
    weight_ref[...] = jnp.where(lat < 16, mixed, final)


def sums(grads, own, rim):
    vmem = pl.BlockSpec(memory_space=VMEM)
    dma = pltpu.SemaphoreType.DMA
    return pl.pallas_call(
        sum_kernel,
        out_shape=(
            jax.ShapeDtypeStruct((ROWS, COLS, C), BF16),
            jax.ShapeDtypeStruct((16, C), F32),
        ),
        in_specs=[vmem] * 3,
        out_specs=(vmem,) * 2,
        scratch_shapes=[
            VMEM((2, 4, CHUNK, C), BF16),
            VMEM((2, 3, CHUNK, C), BF16),
            VMEM((2, 3, CHUNK, C), BF16),
            VMEM((2, CHUNK + 32, C), F32),
            VMEM((2, 8, 32, C), BF16),
            VMEM((2, 7, 32, C), BF16),
            VMEM((2, 32, C), BF16),
            VMEM((8, 16, C), BF16),
            VMEM((2, ROWS, COLS, C), BF16),
            VMEM((6, COLS, C), BF16),
            VMEM((48, C), F32),
            dma((2,)),
            dma((2,)),
            dma((2, 3)),
            dma((2, 3)),
            dma((2, 7)),
            dma((2, 7)),
            dma((2, 4)),
            dma((8,)),
            dma((8,)),
            dma((8,)),
        ],
        compiler_params=pltpu.CompilerParams(
            collective_id=1, has_side_effects=True, vmem_limit_bytes=LIMIT
        ),
    )(grads.reshape(2, 8, CHUNK, C), own, rim)


def on_device(tokens, w_qkv, w_out, w_disco, psi, reach, key_bias, cotangent):
    frame = halo(tokens)
    mixed_out, own, rim, grads = block(
        frame.reshape(FRAME, C), cotangent, w_qkv, w_out, w_disco, psi, reach, key_bias
    )
    input_grad, lines = sums(grads, own, rim)
    size = 9 * C // 2
    first = lax.rem(lax.axis_index("lon"), 2) * size
    weight_grads = lax.dynamic_slice_in_dim(lines[:9].reshape(-1), first, size, 0)
    return (mixed_out, input_grad, weight_grads)


def solution(mesh):
    placed = (
        P("lat", "lon", None),
        P(),
        P(),
        P(),
        P("lat", None),
        P("lat"),
        P(),
        P("lat", "lon", None),
    )
    return jax.shard_map(
        on_device,
        mesh=mesh,
        in_specs=placed,
        out_specs=(P("lat", "lon", None), P("lat", "lon", None), P(("lat", "lon"))),
        check_vma=False,
    )
```

time: 403 us -> 84.8 us (0.21)
  the two profiles are of different devices: /device:TPU:1 before, /device:TPU:7 now
where the time goes in v1:
time: 84.8 us; the launch traced here: 84.5 us
  Pallas kernels  79.4 us (94%)
  local copies, waits for them, and re-layouts  4.37 us (5%)
    pallas_call x1, Pallas kernels, sums(): pl.pallas_call(sum_kernel, out_shape=(jax.ShapeDtypeStruct((ROWS, COLS, C...  50 us
    pallas_call x1, Pallas kernels, halo(): pl.pallas_call(halo_kernel, out_shape=jax.ShapeDtypeStruct((ROWS + 2, SPA...  20.5 us
    pallas_call x1, Pallas kernels, block(): pl.pallas_call(block_kernel, out_shape=(jax.ShapeDtypeStruct((ROWS, COLS,...  9.01 us
    unnamed x2, local copies, waits for them, and re-layouts  2.96 us

profile of v1, /device:TPU:7, one launch (start us, length us, event | category | flops | bytes accessed | tf_op | source)
XLA Modules:
  0.0 84.5 jit_solution(856742378800795152)
XLA Ops:
  0.6 20.5 %shard_map.103 = bf16[6,96,384]{2,1,0:T(8,128)(2,1)} custom-call(bf16[4,32,384]{2,1,0:T(8,128)(2,1)} %tokens_ref.1), custom_call_target="tpu_custom_call" | custom-call | tf_op jit(solution)/shard_map/pallas_call | solution.py:100
  21.1 1.4 %copy.11.bias_ref = f32[128,8]{1,0:T(8,128)} copy(f32[128,8]{0,1:T(8,128)} %param.14) | data formatting | bytes 8192 | tf_op args[6]
  22.5 9.0 %shard_map.104 = (bf16[4,32,384]{2,1,0:T(8,128)(2,1)}, f32[4,32,384]{2,1,0:T(8,128)}, bf16[6,96,384]{2,1,0:T(8,128)(2,1)}, bf16[2,1152,384]{2,1,0:T(8,128)(2,1)}) custom-call(bf16[576,384]{1,0:T(8,128)(2,1)} %bitcast.4, bf16[4,32,384]{2,1,0:T(8,128)(2,1)} %cot_ref.1, bf16[384,1152]{1,0:T(8,128)(2,1)} %w_qkv_ref.1, bf16[384,384]{1,0:T(8,128)(2,1)} %w_out_ref.1, ...), custom_call_target="tpu_custom_call" | custom-call | tf_op jit(solution)/shard_map/pallas_call | solution.py:253
  31.5 50.0 %shard_map.105 = (bf16[4,32,384]{2,1,0:T(8,128)(2,1)}, f32[16,384]{1,0:T(8,128)}) custom-call(bf16[2,8,144,384]{3,2,1,0:T(8,128)(2,1)} %bitcast.3, f32[4,32,384]{2,1,0:T(8,128)} %get-tuple-element.11.own_ref, bf16[6,96,384]{2,1,0:T(8,128)(2,1)} %get-tuple-element.12.rim_ref), custom_call_target="tpu_custom_call" | custom-call | tf_op jit(solution)/shard_map/pallas_call | solution.py:518
  81.5 0.7 reshape.17
  82.2 0.7 dynamic_slice.3
  82.9 1.5 %copy.13 = bf16[4,32,384]{2,1,0:T(8,128)(2,1)} copy(bf16[4,32,384]{2,1,0:T(8,128)(2,1)} %get-tuple-element.19) | data formatting | bytes 196608

commit v2 on v1

v2 whole, which is shorter than its diff:
```python
import jax
import jax.numpy as jnp
from jax import lax
from jax.experimental import pallas as pl
from jax.experimental.pallas import tpu as pltpu
from jax.sharding import PartitionSpec as P

HEADS = 8
HEAD_DIM = 48
C = 384
ROWS = 4
COLS = 32
SPAN = 3 * COLS
FRAME = (ROWS + 2) * SPAN
CELLS = ROWS * COLS
LATS = 32
LONS = 16
CHUNK = 144
SCALING = HEAD_DIM ** (-0.5)
FAR = -1e30
MESH = pl.DeviceIdType.MESH
BF16 = jnp.bfloat16
F32 = jnp.float32
VMEM = pltpu.VMEM
LIMIT = 56 * 1024 * 1024


def nn(left, right):
    return lax.dot_general(left, right, (((1,), (0,)), ((), ())), preferred_element_type=F32)


def nt(left, right):
    return lax.dot_general(left, right, (((1,), (1,)), ((), ())), preferred_element_type=F32)


def tn(left, right):
    return lax.dot_general(left, right, (((0,), (0,)), ((), ())), preferred_element_type=F32)


def place():
    return lax.axis_index("lat"), lax.axis_index("lon")


def neighbours(lat, lon):
    found = []
    for row_step in (-1, 0, 1):
        for col_step in (-1, 0, 1):
            if row_step or col_step:
                target = (
                    lax.rem(lat + row_step + LATS, LATS),
                    lax.rem(lon + col_step + LONS, LONS),
                )
                found.append((row_step, col_step, target))
    return found


def to_chip(y, z, x, core):
    return (y * 4 + z // 2, x * 4 + lax.rem(z, 2) * 2 + core)


def remote(src, dst, send, recv, target):
    return pltpu.make_async_remote_copy(
        src_ref=src,
        dst_ref=dst,
        send_sem=send,
        recv_sem=recv,
        device_id=target,
        device_id_type=MESH,
    )


def whole_kernel(
    tokens_hbm,
    cot_hbm,
    w_qkv_hbm,
    w_out_hbm,
    w_disco_hbm,
    psi_ref,
    reach_ref,
    bias_ref,
    mixed_ref,
    input_ref,
    last_in,
    frame,
    cot_ref,
    w_qkv,
    w_out,
    w_disco,
    perm_x,
    perm_a,
    perm_b,
    kv_ref,
    canvas,
    probs_ref,
    shifted,
    mix_in,
    dq_ref,
    gs_ref,
    grads,
    own_ref,
    rim_ref,
    pair_in,
    x_out,
    x_in,
    total_ref,
    z_out,
    z_in,
    last_out,
    rim_in,
    line_in,
    load_sem,
    halo_send,
    halo_recv,
    pair_send,
    pair_recv,
    x_send,
    x_recv,
    z_send,
    z_recv,
    last_send,
    last_recv,
    rim_send,
    rim_recv,
):
    lat, lon = place()
    y, x, core = lat // 4, lon // 4, lax.rem(lon, 2)
    z = lax.rem(lat, 4) * 2 + lax.rem(lon, 4) // 2
    other = 1 - core

    loads = [
        pltpu.make_async_copy(tokens_hbm, frame.at[pl.ds(1, ROWS), pl.ds(COLS, COLS)], load_sem.at[0]),
        pltpu.make_async_copy(w_qkv_hbm, w_qkv, load_sem.at[1]),
        pltpu.make_async_copy(cot_hbm, cot_ref, load_sem.at[2]),
        pltpu.make_async_copy(w_out_hbm, w_out, load_sem.at[3]),
        pltpu.make_async_copy(w_disco_hbm, w_disco, load_sem.at[4]),
    ]
    for load in loads:
        load.start()

    around = neighbours(lat, lon)
    pair_peer = (lat, lon + 1 - 2 * core)
    x_peers = []
    for d in range(1, 4):
        there, back = lax.rem(x + d, 4), lax.rem(x + 4 - d, 4)
        x_peers.append((there, to_chip(y, z, there, core), to_chip(y, z, back, core)))
    z_peers = []
    for d in range(1, 8):
        there, back = lax.rem(z + d, 8), lax.rem(z + 8 - d, 8)
        z_peers.append((there, to_chip(y, there, x, core), to_chip(y, back, x, core)))
    owners = {}
    for job in range(2):
        for half in range(2):
            for to_core in range(2):
                row = (4 * job + half) + 2 * core
                mine = (row == y) & (core == to_core)
                owners[job, half, to_core] = (to_chip(row, z, x, to_core), mine)
    from_core = lax.rem(y, 4) // 2
    sources = []
    for k in range(8):
        mine = (y == k) & (core == from_core)
        sources.append((to_chip(k, z, x, from_core), mine))

    barrier = pltpu.get_barrier_semaphore()

    def hail(target):
        pl.semaphore_signal(barrier, inc=1, device_id=target, device_id_type=MESH)

    for _, _, target in around:
        hail(target)
    hail(pair_peer)
    for _, _, back in x_peers + z_peers:
        hail(back)
    for target, mine in sources:

        @pl.when(jnp.logical_not(mine))
        def _():
            hail(target)

    expected = 8 + 1 + 3 + 7 + 8 - jnp.where(core == from_core, 1, 0)
    pl.semaphore_wait(barrier, expected)

    halo_copies = []
    for idx, (row_step, col_step, target) in enumerate(around):
        if row_step == -1:
            src, dst_rows = tokens_hbm.at[pl.ds(0, 1)], pl.ds(ROWS + 1, 1)
        elif row_step == 1:
            src, dst_rows = tokens_hbm.at[pl.ds(ROWS - 1, 1)], pl.ds(0, 1)
        else:
            src, dst_rows = tokens_hbm, pl.ds(1, ROWS)
        copy = remote(
            src,
            frame.at[dst_rows, pl.ds((1 - col_step) * COLS, COLS)],
            halo_send.at[idx],
            halo_recv.at[idx],
            target,
        )
        copy.start()
        halo_copies.append(copy)

    def ones_where(equal):
        return jnp.where(equal, 1.0, 0.0).astype(BF16)

    pos = lax.broadcasted_iota(jnp.int32, (C, 128), 0)
    lane = lax.broadcasted_iota(jnp.int32, (C, 128), 1)
    pos_z = lax.rem(pos // 6, 8)
    pos_y = (pos // 192) * 2 + lax.rem(pos // 3, 2)
    origin = 3 * (
        pos_y * 32 + (pos_z // 2) * 8 + lax.rem(pos // 48, 4) * 2 + lax.rem(pos_z, 2)
    ) + lax.rem(pos, 3)
    for t in range(3):
        perm_x[:, 128 * t : 128 * (t + 1)] = ones_where(lane + 128 * t == origin)
    pos = lax.broadcasted_iota(jnp.int32, (4 * CHUNK, 128), 0)
    lane = lax.broadcasted_iota(jnp.int32, (4 * CHUNK, 128), 1)
    pos_z = lax.rem(pos // 18, 8)
    origin = (
        288 * lax.rem(pos // 9, 2)
        + 72 * (pos_z // 2)
        + 18 * (pos // 144)
        + 9 * lax.rem(pos_z, 2)
        + lax.rem(pos, 9)
    )
    for t in range(5):
        perm_a[:, 128 * t : 128 * (t + 1)] = ones_where(lane + 128 * t == origin)
        perm_b[:, 128 * t : 128 * (t + 1)] = ones_where(lane + 128 * t - 64 == origin)

    stack = HEADS * COLS
    head_mask = ones_where(
        lax.broadcasted_iota(jnp.int32, (stack, C), 0) // COLS
        == lax.broadcasted_iota(jnp.int32, (stack, C), 1) // HEAD_DIM
    )
    lane_head = lax.broadcasted_iota(jnp.int32, (COLS, C), 1) // HEAD_DIM
    distance = jnp.abs(
        lax.broadcasted_iota(jnp.int32, (SPAN, stack), 0)
        - COLS
        - lax.rem(lax.broadcasted_iota(jnp.int32, (SPAN, stack), 1), COLS)
    )
    stack_head = lax.broadcasted_iota(jnp.int32, (1, stack), 1) // COLS
    bias_lane = lax.broadcasted_iota(jnp.int32, (HEADS, LATS * ROWS), 1)
    bias_rows = []
    for k in range(ROWS + 2):
        global_row = lat * ROWS - 1 + k
        clamped = jnp.clip(global_row, 0, LATS * ROWS - 1)
        biases = jnp.sum(
            jnp.where(bias_lane == clamped, bias_ref[...], 0.0), axis=1, keepdims=True
        )
        line = jnp.zeros((1, stack), F32)
        for h in range(HEADS):
            line = jnp.where(stack_head == h, biases[h : h + 1], line)
        valid = (global_row >= 0) & (global_row < LATS * ROWS)
        bias_rows.append(jnp.where(valid, line, FAR))

    for load in loads:
        load.wait()
    x_own = frame[1 : ROWS + 1, COLS : 2 * COLS].reshape(CELLS, C)
    cot = cot_ref[...].reshape(CELLS, C)
    queries = nn(x_own, w_qkv[:, :C]).astype(BF16)
    upstream = nt(cot, w_out[...]).astype(BF16)
    gs_ref[...] = nt(cot, w_disco[...]).astype(BF16).astype(F32)
    own_turned = nt(perm_x[...], x_own).astype(BF16)
    canvas[...] = jnp.zeros_like(canvas)

    for copy in halo_copies:
        copy.wait()

    @pl.when(lat == 0)
    def _():
        frame[0] = jnp.zeros((SPAN, C), BF16)

    @pl.when(lat == LATS - 1)
    def _():
        frame[ROWS + 1] = jnp.zeros((SPAN, C), BF16)

    for r in range(ROWS + 2):
        kv_ref[r * SPAN : (r + 1) * SPAN] = nn(frame[r], w_qkv[:, C:]).astype(BF16)

    for r in range(ROWS + 2):
        wide = frame[r, 16:80].astype(F32)
        shifted[0, r] = pltpu.roll(wide, 1, 0)[16:48]
        shifted[1, r] = wide[16:48]
        shifted[2, r] = pltpu.roll(wide, 63, 0)[16:48]
    for r in range(ROWS):
        for k in range(2):
            total = jnp.zeros((COLS, C), F32)
            for a in range(3):
                for b in range(3):
                    total = total + psi_ref[r, 9 * k + 3 * a + b] * shifted[b, r + a]
            mix_in[r * COLS : (r + 1) * COLS, (k + 1) * C : (k + 2) * C] = total.astype(BF16)

    def fold_heads(wide):
        total = jnp.zeros((COLS, C), F32)
        for h in range(HEADS):
            total = jnp.where(lane_head == h, wide[h * COLS : (h + 1) * COLS], total)
        return total

    def all_heads(source, r):
        return jnp.concatenate([source[r * COLS : (r + 1) * COLS]] * HEADS, axis=0) * head_mask

    for r in range(ROWS):
        keys_at = slice(r * SPAN, (r + 3) * SPAN)
        keys, values = kv_ref[keys_at, :C], kv_ref[keys_at, C:]
        outside = jnp.where(distance <= reach_ref[r], 0.0, FAR)
        added = jnp.concatenate([outside + bias_rows[r + a] for a in range(3)], axis=0)
        logits = nt(keys, all_heads(queries, r)) * SCALING + added
        logits = logits - jnp.max(logits, axis=0, keepdims=True)
        probs = jnp.exp(logits)
        probs = probs * (1.0 / jnp.sum(probs, axis=0, keepdims=True))
        probs_ref[r] = probs
        attended = fold_heads(tn(probs.astype(BF16), values))
        mix_in[r * COLS : (r + 1) * COLS, :C] = attended.astype(BF16)

    turned = nt(perm_a[...], mix_in[:, :640]).astype(BF16)
    grads[1, 0:4] = nn(turned, cot).astype(BF16).reshape(4, CHUNK, C)
    turned = nt(perm_b[...], mix_in[:, 512:]).astype(BF16)
    grads[1, 4:8] = nn(turned, cot).astype(BF16).reshape(4, CHUNK, C)

    def pair_copy(job):
        return remote(
            grads.at[job, pl.ds(other * 4, 4)],
            pair_in.at[job],
            pair_send.at[job],
            pair_recv.at[job],
            pair_peer,
        )

    def x_copy(job, d):
        return remote(
            x_out.at[job, d], x_in.at[job, d], x_send.at[job, d], x_recv.at[job, d], x_peers[d][1]
        )

    def z_copies(job):
        return [
            remote(
                z_out.at[job, there],
                z_in.at[job, d],
                z_send.at[job, d],
                z_recv.at[job, d],
                target,
            )
            for d, (there, target, _) in enumerate(z_peers)
        ]

    def last_copy(job, half, to_core):
        return remote(
            last_out.at[job, pl.ds(half * 16, 16)],
            last_in.at[y],
            last_send.at[job, 2 * half + to_core],
            last_recv.at[y],
            owners[job, half, to_core][0],
        )

    def send_x(job):
        pair_copy(job).wait()
        for d, (there, _, _) in enumerate(x_peers):
            added = grads[job, core * 4 + there].astype(F32) + pair_in[job, there].astype(F32)
            x_out[job, d] = added.astype(BF16)
            x_copy(job, d).start()

    row_ids = lax.broadcasted_iota(jnp.int32, (16, C), 0)

    def send_z(job):
        total = grads[job, core * 4 + x].astype(F32) + pair_in[job, x].astype(F32)
        for d in range(3):
            x_copy(job, d).wait()
            total = total + x_in[job, d].astype(F32)
        total_ref[job, 0:8] = jnp.zeros((8, C), F32)
        total_ref[job, 8 : 8 + CHUNK] = total
        total_ref[job, 8 + CHUNK : 32 + CHUNK] = jnp.zeros((24, C), F32)
        for k in range(8):
            for half in range(2):
                if job == 1:
                    first = 8 + 18 * k + 9 * half
                    lines = total_ref[job, first : first + 16]
                else:
                    first = 8 + 6 * k + 3 * half
                    parts = [total_ref[job, first + 45 * m : first + 45 * m + 16] for m in range(3)]
                    lines = jnp.where(row_ids < 3, parts[0], jnp.where(row_ids < 6, parts[1], parts[2]))
                z_out[job, k, half * 16 : half * 16 + 16] = lines.astype(BF16)
        for copy in z_copies(job):
            copy.start()

    def send_last(job):
        total = z_out[job, z].astype(F32)
        for d, copy in enumerate(z_copies(job)):
            copy.wait()
            total = total + z_in[job, d].astype(F32)
        last_out[job] = total.astype(BF16)
        for half in range(2):
            for to_core in range(2):
                mine = owners[job, half, to_core][1]

                @pl.when(jnp.logical_not(mine))
                def _():
                    last_copy(job, half, to_core).start()

                @pl.when(mine)
                def _():
                    last_in[y] = last_out[job, half * 16 : half * 16 + 16]

    pair_copy(1).start()

    def backward(r):
        keys_at = slice(r * SPAN, (r + 3) * SPAN)
        keys, values = kv_ref[keys_at, :C], kv_ref[keys_at, C:]
        q_heads, u_heads = all_heads(queries, r), all_heads(upstream, r)
        probs = probs_ref[r]
        grad_prob = nt(values, u_heads).astype(BF16).astype(F32)
        mean = jnp.sum(probs * grad_prob, axis=0, keepdims=True)
        grad_logit = (probs * (grad_prob - mean)).astype(BF16)
        cells = slice(r * COLS, (r + 1) * COLS)
        dq_ref[cells] = (fold_heads(tn(grad_logit, keys)) * SCALING).astype(BF16)
        canvas[keys_at, :C] += nn(grad_logit, q_heads) * SCALING
        canvas[keys_at, C:] += nn(probs.astype(BF16), u_heads)

    backward(0)
    backward(1)
    send_x(1)
    backward(2)
    backward(3)

    grad_query = dq_ref[...]
    kv_part = canvas[...].astype(BF16)
    query_weight = nn(own_turned, grad_query).astype(BF16)
    frame_turned = nt(perm_x[...], frame[...].reshape(FRAME, C)).astype(BF16)
    kv_weight = nn(frame_turned, kv_part).astype(BF16)
    for c in range(8):
        lines = slice(48 * c, 48 * (c + 1))
        grads[0, c, 0:48] = query_weight[lines]
        grads[0, c, 48:96] = kv_weight[lines, :C]
        grads[0, c, 96:144] = kv_weight[lines, C:]
    pair_copy(0).start()

    canvas[:, :C] = nt(kv_part, w_qkv[:, C:])
    send_x(0)
    query_part = nt(grad_query, w_qkv[:, :C])
    margin = jnp.zeros((16, C), F32)
    for row in range(ROWS + 2):
        spread = jnp.zeros((64, C), F32)
        for b in range(3):
            total = jnp.zeros((COLS, C), F32)
            for a in range(3):
                r = row - a
                if 0 <= r < ROWS:
                    for k in range(2):
                        total = total + (
                            psi_ref[r, 9 * k + 3 * a + b]
                            * gs_ref[r * COLS : (r + 1) * COLS, k * C : (k + 1) * C]
                        )
            total = jnp.concatenate([margin, total, margin], axis=0)
            spread = spread + (total if b == 1 else pltpu.roll(total, 63 if b == 0 else 1, 0))
        canvas[row * SPAN + 16 : row * SPAN + 80, :C] += spread
    rim_ref[...] = canvas[:, :C].astype(BF16).reshape(ROWS + 2, SPAN, C)
    rim_copies = []
    for idx, (row_step, col_step, target) in enumerate(around):
        if row_step == 0:
            src = rim_ref.at[pl.ds(1, ROWS), pl.ds((1 + col_step) * COLS, COLS)]
            dst = rim_in.at[0 if col_step == -1 else 1]
        else:
            row = 0 if row_step == -1 else ROWS + 1
            src = rim_ref.at[row, pl.ds((1 + col_step) * COLS, COLS)]
            dst = line_in.at[(0 if row_step == -1 else 3) + col_step + 1]
        copy = remote(src, dst, rim_send.at[idx], rim_recv.at[idx], target)
        copy.start()
        rim_copies.append(copy)
    for r in range(ROWS):
        at = (r + 1) * SPAN + COLS
        own_ref[r] = canvas[at : at + COLS, :C] + query_part[r * COLS : (r + 1) * COLS]

    send_z(1)
    mixed = nn(mix_in[:, :C], w_out[...]) + nn(mix_in[:, C:], w_disco[...])
    mixed_ref[...] = mixed.astype(BF16).reshape(ROWS, COLS, C)
    send_z(0)
    send_last(1)

    for copy in rim_copies:
        copy.wait()
    above = jnp.where(lat > 0, 1.0, 0.0)
    below = jnp.where(lat < LATS - 1, 1.0, 0.0)
    for r in range(ROWS):
        summed = own_ref[r] + rim_in[0, r].astype(F32) + rim_in[1, r].astype(F32)
        for side in range(3):
            if r == 0:
                summed = summed + above * line_in[3 + side].astype(F32)
            if r == ROWS - 1:
                summed = summed + below * line_in[side].astype(F32)
        input_ref[r] = summed.astype(BF16)

    send_last(0)
    for k, (source, mine) in enumerate(sources):

        @pl.when(jnp.logical_not(mine))
        def _():
            remote(
                last_out.at[0, pl.ds(0, 16)],
                last_in.at[k],
                last_send.at[0, 0],
                last_recv.at[k],
                source,
            ).wait_recv()

    for (job, half, to_core), (_, mine) in owners.items():

        @pl.when(jnp.logical_not(mine))
        def _():
            last_copy(job, half, to_core).wait_send()


def whole(tokens, cotangent, w_qkv, w_out, w_disco, psi, reach, key_bias):
    vmem = pl.BlockSpec(memory_space=VMEM)
    smem = pl.BlockSpec(memory_space=pltpu.SMEM)
    anywhere = pl.BlockSpec(memory_space=pl.ANY)
    dma = pltpu.SemaphoreType.DMA
    return pl.pallas_call(
        whole_kernel,
        out_shape=(
            jax.ShapeDtypeStruct((ROWS, COLS, C), BF16),
            jax.ShapeDtypeStruct((ROWS, COLS, C), BF16),
            jax.ShapeDtypeStruct((8, 16, C), BF16),
        ),
        in_specs=[anywhere] * 5 + [smem] * 2 + [vmem],
        out_specs=(vmem,) * 3,
        scratch_shapes=[
            VMEM((ROWS + 2, SPAN, C), BF16),
            VMEM((ROWS, COLS, C), BF16),
            VMEM((C, 3 * C), BF16),
            VMEM((C, C), BF16),
            VMEM((2 * C, C), BF16),
            VMEM((C, C), BF16),
            VMEM((4 * CHUNK, 640), BF16),
            VMEM((4 * CHUNK, 640), BF16),
            VMEM((FRAME, 2 * C), BF16),
            VMEM((FRAME, 2 * C), F32),
            VMEM((ROWS, 3 * SPAN, HEADS * COLS), F32),
            VMEM((3, ROWS + 2, COLS, C), F32),
            VMEM((CELLS, 3 * C), BF16),
            VMEM((CELLS, C), BF16),
            VMEM((CELLS, 2 * C), F32),
            VMEM((2, 8, CHUNK, C), BF16),
            VMEM((ROWS, COLS, C), F32),
            VMEM((ROWS + 2, SPAN, C), BF16),
            VMEM((2, 4, CHUNK, C), BF16),
            VMEM((2, 3, CHUNK, C), BF16),
            VMEM((2, 3, CHUNK, C), BF16),
            VMEM((2, CHUNK + 32, C), F32),
            VMEM((2, 8, 32, C), BF16),
            VMEM((2, 7, 32, C), BF16),
            VMEM((2, 32, C), BF16),
            VMEM((2, ROWS, COLS, C), BF16),
            VMEM((6, COLS, C), BF16),
            dma((5,)),
            dma((8,)),
            dma((8,)),
            dma((2,)),
            dma((2,)),
            dma((2, 3)),
            dma((2, 3)),
            dma((2, 7)),
            dma((2, 7)),
            dma((2, 4)),
            dma((8,)),
            dma((8,)),
            dma((8,)),
        ],
        compiler_params=pltpu.CompilerParams(
            collective_id=0, has_side_effects=True, vmem_limit_bytes=LIMIT
        ),
    )(tokens, cotangent, w_qkv, w_out, w_disco, psi, reach, key_bias.T)


def finish_kernel(mixed_in, input_in, lines_ref, mixed_out, input_out, weight_ref):
    mixed_out[...] = mixed_in[...]
    input_out[...] = input_in[...]
    lat, lon = place()
    total = lines_ref[0].astype(F32)
    for k in range(1, 8):
        total = total + lines_ref[k].astype(F32)
    strips = []
    for row in range(9):
        origin = 3 * (row % 3) + row // 3
        line = jnp.where(lat < 16, total[origin : origin + 1], total[row : row + 1])
        strips += [line[:, 128 * t : 128 * (t + 1)] for t in range(3)]
    turned = [pltpu.roll(strip, 64, 1) for strip in strips[13:]]
    left = lax.broadcasted_iota(jnp.int32, (1, 128), 1) < 64
    first_core = lax.rem(lon, 2) == 0
    for j in range(14):
        later = turned[j] if j == 13 else jnp.where(left, turned[j], turned[j + 1])
        strip = jnp.where(first_core, strips[j], later).reshape(128)
        if j < 13:
            weight_ref[128 * j : 128 * (j + 1)] = strip
        else:
            weight_ref[128 * j : 128 * j + 64] = strip[:64]


def finish(mixed, input_grad, lines):
    vmem = pl.BlockSpec(memory_space=VMEM)
    return pl.pallas_call(
        finish_kernel,
        out_shape=(
            jax.ShapeDtypeStruct((ROWS, COLS, C), BF16),
            jax.ShapeDtypeStruct((ROWS, COLS, C), BF16),
            jax.ShapeDtypeStruct((9 * C // 2,), F32),
        ),
        in_specs=[vmem] * 3,
        out_specs=(vmem,) * 3,
    )(mixed, input_grad, lines)


def on_device(tokens, w_qkv, w_out, w_disco, psi, reach, key_bias, cotangent):
    mixed, input_grad, lines = whole(
        tokens, cotangent, w_qkv, w_out, w_disco, psi, reach, key_bias
    )
    return finish(mixed, input_grad, lines)


def solution(mesh):
    placed = (
        P("lat", "lon", None),
        P(),
        P(),
        P(),
        P("lat", None),
        P("lat"),
        P(),
        P("lat", "lon", None),
    )
    return jax.shard_map(
        on_device,
        mesh=mesh,
        in_specs=placed,
        out_specs=(P("lat", "lon", None), P("lat", "lon", None), P(("lat", "lon"))),
        check_vma=False,
    )
```

time: 84.8 us -> 60 us (0.71)
  the two profiles are of different devices: /device:TPU:7 before, /device:TPU:1 now
where the time goes in v2:
time: 60 us; the launch traced here: 59.8 us
  Pallas kernels  59.2 us (99%)
  between operations  0.64 us (1%)
    pallas_call x1, Pallas kernels, whole(): pl.pallas_call(whole_kernel, out_shape=(jax.ShapeDtypeStruct((ROWS, COLS,...  57.5 us
    pallas_call x1, Pallas kernels, finish(): pl.pallas_call(finish_kernel, out_shape=(jax.ShapeDtypeStruct((ROWS, COLS...  1.69 us

profile of v2, /device:TPU:1, one launch (start us, length us, event | category | flops | bytes accessed | tf_op | source)
XLA Modules:
  0.0 59.8 jit_solution(12412543202243794580)
XLA Ops:
  0.6 57.5 %shard_map.103 = (bf16[4,32,384]{2,1,0:T(8,128)(2,1)}, bf16[4,32,384]{2,1,0:T(8,128)(2,1)}, bf16[8,16,384]{2,1,0:T(8,128)(2,1)}) custom-call(bf16[4,32,384]{2,1,0:T(8,128)(2,1)} %tokens_hbm.1, bf16[4,32,384]{2,1,0:T(8,128)(2,1)} %cot_hbm.1, bf16[384,1152]{1,0:T(8,128)(2,1)} %w_qkv_hbm.1, bf16[384,384]{1,0:T(8,128)(2,1)} %w_out_hbm.1, ...), custom_call_target="tpu_custom_call" | custom-call | tf_op jit(solution)/shard_map/pallas_call | solution.py:512
  58.1 1.7 %shard_map.104 = (bf16[4,32,384]{2,1,0:T(8,128)(2,1)}, bf16[4,32,384]{2,1,0:T(8,128)(2,1)}, f32[1728]{0:T(1024)}) custom-call(bf16[4,32,384]{2,1,0:T(8,128)(2,1)} %get-tuple-element.6.mixed_in, bf16[4,32,384]{2,1,0:T(8,128)(2,1)} %get-tuple-element.7.input_in, bf16[8,16,384]{2,1,0:T(8,128)(2,1)} %get-tuple-element.8.lines_ref), custom_call_target="tpu_custom_call" | custom-call | tf_op jit(solution)/shard_map/pallas_call | solution.py:595

commit v3 on v2

--- a/solution.py
+++ b/solution.py
@@ -78,20 +78,26 @@
     psi_ref,
     reach_ref,
     bias_ref,
+    mixed_hbm,
+    input_hbm,
+    last_in,
     mixed_ref,
     input_ref,
-    last_in,
     frame,
     cot_ref,
     w_qkv,
     w_out,
     w_disco,
     perm_x,
-    perm_a,
-    perm_b,
+    perm_od,
+    turned_own,
+    turned_mid,
+    turned_edge,
     kv_ref,
     canvas,
     probs_ref,
+    low_ref,
+    glow_ref,
     shifted,
     mix_in,
     dq_ref,
@@ -103,12 +109,14 @@
     x_out,
     x_in,
     total_ref,
+    pack_ref,
     z_out,
     z_in,
     last_out,
     rim_in,
     line_in,
     load_sem,
+    store_sem,
     halo_send,
     halo_recv,
     pair_send,
@@ -220,8 +228,8 @@
         + lax.rem(pos, 9)
     )
     for t in range(5):
-        perm_a[:, 128 * t : 128 * (t + 1)] = ones_where(lane + 128 * t == origin)
-        perm_b[:, 128 * t : 128 * (t + 1)] = ones_where(lane + 128 * t - 64 == origin)
+        perm_od[0, :, 128 * t : 128 * (t + 1)] = ones_where(lane + 128 * t == origin)
+        perm_od[1, :, 128 * t : 128 * (t + 1)] = ones_where(lane + 128 * t - 64 == origin)
 
     stack = HEADS * COLS
     head_mask = ones_where(
@@ -256,11 +264,18 @@
     queries = nn(x_own, w_qkv[:, :C]).astype(BF16)
     upstream = nt(cot, w_out[...]).astype(BF16)
     gs_ref[...] = nt(cot, w_disco[...]).astype(BF16).astype(F32)
-    own_turned = nt(perm_x[...], x_own).astype(BF16)
+    turned_own[...] = nt(perm_x[...], x_own).astype(BF16)
     canvas[...] = jnp.zeros_like(canvas)
 
-    for copy in halo_copies:
-        copy.wait()
+    sides = [idx for idx, (row_step, _, _) in enumerate(around) if row_step == 0]
+    for idx in sides:
+        halo_copies[idx].wait()
+    middle = frame[1 : ROWS + 1].reshape(ROWS * SPAN, C)
+    kv_ref[SPAN : SPAN + ROWS * SPAN] = nn(middle, w_qkv[:, C:]).astype(BF16)
+    turned_mid[...] = nt(perm_x[...], middle).astype(BF16)
+    for idx, copy in enumerate(halo_copies):
+        if idx not in sides:
+            copy.wait()
 
     @pl.when(lat == 0)
     def _():
@@ -270,8 +285,10 @@
     def _():
         frame[ROWS + 1] = jnp.zeros((SPAN, C), BF16)
 
-    for r in range(ROWS + 2):
-        kv_ref[r * SPAN : (r + 1) * SPAN] = nn(frame[r], w_qkv[:, C:]).astype(BF16)
+    edges = jnp.concatenate([frame[0], frame[ROWS + 1]], axis=0)
+    edge_kv = nn(edges, w_qkv[:, C:]).astype(BF16)
+    kv_ref[:SPAN] = edge_kv[:SPAN]
+    kv_ref[FRAME - SPAN :] = edge_kv[SPAN:]
 
     for r in range(ROWS + 2):
         wide = frame[r, 16:80].astype(F32)
@@ -286,41 +303,63 @@
                     total = total + psi_ref[r, 9 * k + 3 * a + b] * shifted[b, r + a]
             mix_in[r * COLS : (r + 1) * COLS, (k + 1) * C : (k + 2) * C] = total.astype(BF16)
 
-    def fold_heads(wide):
-        total = jnp.zeros((COLS, C), F32)
-        for h in range(HEADS):
-            total = jnp.where(lane_head == h, wide[h * COLS : (h + 1) * COLS], total)
-        return total
+    def fold_heads(weights, channels, rows):
+        folded = []
+        for g in range(2):
+            window = kv_ref[rows, channels + 128 * g : channels + 128 * g + 256]
+            wide = tn(weights[:, 128 * g : 128 * (g + 1)], window)
+            total = jnp.zeros((COLS, 256), F32)
+            for h in range(4):
+                total = jnp.where(
+                    lane_head[:, 128 * g : 128 * g + 256] == 4 * g + h,
+                    wide[h * COLS : (h + 1) * COLS],
+                    total,
+                )
+            folded.append(total)
+        first, second = folded
+        return jnp.concatenate(
+            [first[:, :128], first[:, 128:] + second[:, :128], second[:, 128:]], axis=1
+        )
+
+    def key_rows(r):
+        return slice(r * SPAN, (r + 3) * SPAN)
 
     def all_heads(source, r):
         return jnp.concatenate([source[r * COLS : (r + 1) * COLS]] * HEADS, axis=0) * head_mask
 
-    for r in range(ROWS):
-        keys_at = slice(r * SPAN, (r + 3) * SPAN)
-        keys, values = kv_ref[keys_at, :C], kv_ref[keys_at, C:]
+    q_heads = [all_heads(queries, r) for r in range(ROWS)]
+    u_heads = [all_heads(upstream, r) for r in range(ROWS)]
+    for r in range(ROWS):
         outside = jnp.where(distance <= reach_ref[r], 0.0, FAR)
         added = jnp.concatenate([outside + bias_rows[r + a] for a in range(3)], axis=0)
-        logits = nt(keys, all_heads(queries, r)) * SCALING + added
-        logits = logits - jnp.max(logits, axis=0, keepdims=True)
-        probs = jnp.exp(logits)
+        probs_ref[r] = nt(kv_ref[key_rows(r), :C], q_heads[r]) * SCALING + added
+    for r in range(ROWS):
+        logits = probs_ref[r]
+        probs = jnp.exp(logits - jnp.max(logits, axis=0, keepdims=True))
         probs = probs * (1.0 / jnp.sum(probs, axis=0, keepdims=True))
         probs_ref[r] = probs
-        attended = fold_heads(tn(probs.astype(BF16), values))
-        mix_in[r * COLS : (r + 1) * COLS, :C] = attended.astype(BF16)
-
-    turned = nt(perm_a[...], mix_in[:, :640]).astype(BF16)
-    grads[1, 0:4] = nn(turned, cot).astype(BF16).reshape(4, CHUNK, C)
-    turned = nt(perm_b[...], mix_in[:, 512:]).astype(BF16)
-    grads[1, 4:8] = nn(turned, cot).astype(BF16).reshape(4, CHUNK, C)
-
-    def pair_copy(job):
+        low_ref[r] = probs.astype(BF16)
+    for r in range(ROWS):
+        mix_in[r * COLS : (r + 1) * COLS, :C] = fold_heads(low_ref[r], C, key_rows(r)).astype(BF16)
+
+    def mix_weights(half):
+        window = mix_in[:, pl.ds(pl.multiple_of(512 * half, 128), 640)]
+        turned = nt(perm_od[half], window).astype(BF16)
+        grads[1, pl.ds(4 * half, 4)] = nn(turned, cot).astype(BF16).reshape(4, CHUNK, C)
+
+    def pair_copy(job, step):
+        there = lax.rem(x + step, 4)
         return remote(
-            grads.at[job, pl.ds(other * 4, 4)],
-            pair_in.at[job],
-            pair_send.at[job],
-            pair_recv.at[job],
+            grads.at[job, other * 4 + there],
+            pair_in.at[job, there],
+            pair_send.at[job, step],
+            pair_recv.at[job, step],
             pair_peer,
         )
+
+    def send_pair(job):
+        for step in (2, 1, 3, 0):
+            pair_copy(job, step).start()
 
     def x_copy(job, d):
         return remote(
@@ -341,7 +380,7 @@
 
     def last_copy(job, half, to_core):
         return remote(
-            last_out.at[job, pl.ds(half * 16, 16)],
+            last_out.at[job, pl.ds(half * 32, 32)],
             last_in.at[y],
             last_send.at[job, 2 * half + to_core],
             last_recv.at[y],
@@ -349,15 +388,15 @@
         )
 
     def send_x(job):
-        pair_copy(job).wait()
-        for d, (there, _, _) in enumerate(x_peers):
+        for d in (1, 0, 2):
+            there = x_peers[d][0]
+            pair_copy(job, d + 1).wait()
             added = grads[job, core * 4 + there].astype(F32) + pair_in[job, there].astype(F32)
             x_out[job, d] = added.astype(BF16)
             x_copy(job, d).start()
 
-    row_ids = lax.broadcasted_iota(jnp.int32, (16, C), 0)
-
     def send_z(job):
+        pair_copy(job, 0).wait()
         total = grads[job, core * 4 + x].astype(F32) + pair_in[job, x].astype(F32)
         for d in range(3):
             x_copy(job, d).wait()
@@ -367,14 +406,20 @@
         total_ref[job, 8 + CHUNK : 32 + CHUNK] = jnp.zeros((24, C), F32)
         for k in range(8):
             for half in range(2):
-                if job == 1:
-                    first = 8 + 18 * k + 9 * half
-                    lines = total_ref[job, first : first + 16]
-                else:
-                    first = 8 + 6 * k + 3 * half
-                    parts = [total_ref[job, first + 45 * m : first + 45 * m + 16] for m in range(3)]
-                    lines = jnp.where(row_ids < 3, parts[0], jnp.where(row_ids < 6, parts[1], parts[2]))
-                z_out[job, k, half * 16 : half * 16 + 16] = lines.astype(BF16)
+                for t in range(3):
+                    lanes = slice(128 * t, 128 * (t + 1))
+                    to = 64 * k + 32 * half + 9 * t
+                    if job == 1:
+                        first = 8 + 18 * k + 9 * half
+                        pack_ref[job, to : to + 16] = total_ref[job, first : first + 16, lanes]
+                    else:
+                        for m in range(3):
+                            first = 8 + 48 * m + 6 * k + 3 * half
+                            pack_ref[job, to + 3 * m : to + 3 * m + 8] = total_ref[
+                                job, first : first + 8, lanes
+                            ]
+        for k in range(8):
+            z_out[job, k] = pack_ref[job, 64 * k : 64 * k + 64].astype(BF16)
         for copy in z_copies(job):
             copy.start()
 
@@ -394,40 +439,44 @@
 
                 @pl.when(mine)
                 def _():
-                    last_in[y] = last_out[job, half * 16 : half * 16 + 16]
-
-    pair_copy(1).start()
-
-    def backward(r):
-        keys_at = slice(r * SPAN, (r + 3) * SPAN)
-        keys, values = kv_ref[keys_at, :C], kv_ref[keys_at, C:]
-        q_heads, u_heads = all_heads(queries, r), all_heads(upstream, r)
+                    last_in[y] = last_out[job, half * 32 : half * 32 + 32]
+
+    mix_weights(other)
+    send_pair(1)
+    mix_weights(core)
+
+    for r in range(ROWS):
+        grad_prob = nt(kv_ref[key_rows(r), C:], u_heads[r]).astype(BF16).astype(F32)
         probs = probs_ref[r]
-        grad_prob = nt(values, u_heads).astype(BF16).astype(F32)
         mean = jnp.sum(probs * grad_prob, axis=0, keepdims=True)
-        grad_logit = (probs * (grad_prob - mean)).astype(BF16)
+        glow_ref[r] = (probs * (grad_prob - mean)).astype(BF16)
+    send_x(1)
+    for r in range(ROWS):
         cells = slice(r * COLS, (r + 1) * COLS)
-        dq_ref[cells] = (fold_heads(tn(grad_logit, keys)) * SCALING).astype(BF16)
-        canvas[keys_at, :C] += nn(grad_logit, q_heads) * SCALING
-        canvas[keys_at, C:] += nn(probs.astype(BF16), u_heads)
-
-    backward(0)
-    backward(1)
-    send_x(1)
-    backward(2)
-    backward(3)
+        dq_ref[cells] = (fold_heads(glow_ref[r], 0, key_rows(r)) * SCALING).astype(BF16)
+        canvas[key_rows(r), :C] += nn(glow_ref[r], q_heads[r]) * SCALING
+        canvas[key_rows(r), C:] += nn(low_ref[r], u_heads[r])
 
     grad_query = dq_ref[...]
     kv_part = canvas[...].astype(BF16)
-    query_weight = nn(own_turned, grad_query).astype(BF16)
-    frame_turned = nt(perm_x[...], frame[...].reshape(FRAME, C)).astype(BF16)
-    kv_weight = nn(frame_turned, kv_part).astype(BF16)
-    for c in range(8):
-        lines = slice(48 * c, 48 * (c + 1))
-        grads[0, c, 0:48] = query_weight[lines]
-        grads[0, c, 48:96] = kv_weight[lines, :C]
-        grads[0, c, 96:144] = kv_weight[lines, C:]
-    pair_copy(0).start()
+    kv_middle = kv_part[SPAN : SPAN + ROWS * SPAN]
+    kv_edges = jnp.concatenate([kv_part[:SPAN], kv_part[FRAME - SPAN :]], axis=0)
+    turned_edge[...] = nt(perm_x[...], edges).astype(BF16)
+
+    def token_weights(half):
+        lines = pl.ds(pl.multiple_of(192 * half, 64), 192)
+        query_weight = nn(turned_own[lines], grad_query).astype(BF16)
+        kv_weight = nn(turned_mid[lines], kv_middle) + nn(turned_edge[lines], kv_edges)
+        kv_weight = kv_weight.astype(BF16)
+        for c in range(4):
+            part = slice(48 * c, 48 * (c + 1))
+            grads[0, 4 * half + c, 0:48] = query_weight[part]
+            grads[0, 4 * half + c, 48:96] = kv_weight[part, :C]
+            grads[0, 4 * half + c, 96:144] = kv_weight[part, C:]
+
+    token_weights(other)
+    send_pair(0)
+    token_weights(core)
 
     canvas[:, :C] = nt(kv_part, w_qkv[:, C:])
     send_x(0)
@@ -468,6 +517,8 @@
     send_z(1)
     mixed = nn(mix_in[:, :C], w_out[...]) + nn(mix_in[:, C:], w_disco[...])
     mixed_ref[...] = mixed.astype(BF16).reshape(ROWS, COLS, C)
+    mixed_store = pltpu.make_async_copy(mixed_ref, mixed_hbm, store_sem.at[0])
+    mixed_store.start()
     send_z(0)
     send_last(1)
 
@@ -483,6 +534,8 @@
             if r == ROWS - 1:
                 summed = summed + below * line_in[side].astype(F32)
         input_ref[r] = summed.astype(BF16)
+    input_store = pltpu.make_async_copy(input_ref, input_hbm, store_sem.at[1])
+    input_store.start()
 
     send_last(0)
     for k, (source, mine) in enumerate(sources):
@@ -490,7 +543,7 @@
         @pl.when(jnp.logical_not(mine))
         def _():
             remote(
-                last_out.at[0, pl.ds(0, 16)],
+                last_out.at[0, pl.ds(0, 32)],
                 last_in.at[k],
                 last_send.at[0, 0],
                 last_recv.at[k],
@@ -502,6 +555,9 @@
         @pl.when(jnp.logical_not(mine))
         def _():
             last_copy(job, half, to_core).wait_send()
+
+    mixed_store.wait()
+    input_store.wait()
 
 
 def whole(tokens, cotangent, w_qkv, w_out, w_disco, psi, reach, key_bias):
@@ -514,22 +570,28 @@
         out_shape=(
             jax.ShapeDtypeStruct((ROWS, COLS, C), BF16),
             jax.ShapeDtypeStruct((ROWS, COLS, C), BF16),
-            jax.ShapeDtypeStruct((8, 16, C), BF16),
+            jax.ShapeDtypeStruct((8, 32, 128), BF16),
         ),
         in_specs=[anywhere] * 5 + [smem] * 2 + [vmem],
-        out_specs=(vmem,) * 3,
+        out_specs=(anywhere, anywhere, vmem),
         scratch_shapes=[
+            VMEM((ROWS, COLS, C), BF16),
+            VMEM((ROWS, COLS, C), BF16),
             VMEM((ROWS + 2, SPAN, C), BF16),
             VMEM((ROWS, COLS, C), BF16),
             VMEM((C, 3 * C), BF16),
             VMEM((C, C), BF16),
             VMEM((2 * C, C), BF16),
             VMEM((C, C), BF16),
-            VMEM((4 * CHUNK, 640), BF16),
-            VMEM((4 * CHUNK, 640), BF16),
+            VMEM((2, 4 * CHUNK, 640), BF16),
+            VMEM((C, CELLS), BF16),
+            VMEM((C, ROWS * SPAN), BF16),
+            VMEM((C, 2 * SPAN), BF16),
             VMEM((FRAME, 2 * C), BF16),
             VMEM((FRAME, 2 * C), F32),
             VMEM((ROWS, 3 * SPAN, HEADS * COLS), F32),
+            VMEM((ROWS, 3 * SPAN, HEADS * COLS), BF16),
+            VMEM((ROWS, 3 * SPAN, HEADS * COLS), BF16),
             VMEM((3, ROWS + 2, COLS, C), F32),
             VMEM((CELLS, 3 * C), BF16),
             VMEM((CELLS, C), BF16),
@@ -541,16 +603,18 @@
             VMEM((2, 3, CHUNK, C), BF16),
             VMEM((2, 3, CHUNK, C), BF16),
             VMEM((2, CHUNK + 32, C), F32),
-            VMEM((2, 8, 32, C), BF16),
-            VMEM((2, 7, 32, C), BF16),
-            VMEM((2, 32, C), BF16),
+            VMEM((2, 8 * 64 + 16, 128), F32),
+            VMEM((2, 8, 64, 128), BF16),
+            VMEM((2, 7, 64, 128), BF16),
+            VMEM((2, 64, 128), BF16),
             VMEM((2, ROWS, COLS, C), BF16),
             VMEM((6, COLS, C), BF16),
             dma((5,)),
+            dma((2,)),
             dma((8,)),
             dma((8,)),
-            dma((2,)),
-            dma((2,)),
+            dma((2, 4)),
+            dma((2, 4)),
             dma((2, 3)),
             dma((2, 3)),
             dma((2, 7)),
@@ -576,8 +640,9 @@
     strips = []
     for row in range(9):
         origin = 3 * (row % 3) + row // 3
-        line = jnp.where(lat < 16, total[origin : origin + 1], total[row : row + 1])
-        strips += [line[:, 128 * t : 128 * (t + 1)] for t in range(3)]
+        for t in range(3):
+            at, late = 9 * t + origin, 9 * t + row
+            strips.append(jnp.where(lat < 16, total[at : at + 1], total[late : late + 1]))
     turned = [pltpu.roll(strip, 64, 1) for strip in strips[13:]]
     left = lax.broadcasted_iota(jnp.int32, (1, 128), 1) < 64
     first_core = lax.rem(lon, 2) == 0

time: 60 us -> 56.6 us (0.943)
  Pallas kernels: 59.2 us -> 55.8 us
    pallas_call x1, Pallas kernels: 57.5 us -> 54.2 us  [whole(): pl.pallas_call(whole_kernel, out_shape=(jax.ShapeDtypeStruct((ROWS, COLS,...]
where the time goes in v3:
time: 56.6 us; the launch traced here: 56.5 us
  Pallas kernels  55.8 us (99%)
  between operations  0.64 us (1%)
    pallas_call x1, Pallas kernels, whole(): pl.pallas_call(whole_kernel, out_shape=(jax.ShapeDtypeStruct((ROWS, COLS,...  54.2 us
    pallas_call x1, Pallas kernels, finish(): pl.pallas_call(finish_kernel, out_shape=(jax.ShapeDtypeStruct((ROWS, COLS...  1.64 us

profile of v3, /device:TPU:1, one launch (start us, length us, event | category | flops | bytes accessed | tf_op | source)
XLA Modules:
  0.0 56.5 jit_solution(14556470015951697244)
XLA Ops:
  0.6 54.2 %shard_map.103 = (bf16[4,32,384]{2,1,0:T(8,128)(2,1)}, bf16[4,32,384]{2,1,0:T(8,128)(2,1)}, bf16[8,32,128]{2,1,0:T(8,128)(2,1)}) custom-call(bf16[4,32,384]{2,1,0:T(8,128)(2,1)} %tokens_hbm.1, bf16[4,32,384]{2,1,0:T(8,128)(2,1)} %cot_hbm.1, bf16[384,1152]{1,0:T(8,128)(2,1)} %w_qkv_hbm.1, bf16[384,384]{1,0:T(8,128)(2,1)} %w_out_hbm.1, ...), custom_call_target="tpu_custom_call" | custom-call | tf_op jit(solution)/shard_map/pallas_call | solution.py:568
  54.8 1.6 %shard_map.104 = (bf16[4,32,384]{2,1,0:T(8,128)(2,1)}, bf16[4,32,384]{2,1,0:T(8,128)(2,1)}, f32[1728]{0:T(1024)}) custom-call(bf16[4,32,384]{2,1,0:T(8,128)(2,1)} %get-tuple-element.6.mixed_in, bf16[4,32,384]{2,1,0:T(8,128)(2,1)} %get-tuple-element.7.input_in, bf16[8,32,128]{2,1,0:T(8,128)(2,1)} %get-tuple-element.8.lines_ref), custom_call_target="tpu_custom_call" | custom-call | tf_op jit(solution)/shard_map/pallas_call | solution.py:660

commit v4 on v3

--- a/solution.py
+++ b/solution.py
@@ -115,6 +115,7 @@
     last_out,
     rim_in,
     line_in,
+    far_sem,
     load_sem,
     store_sem,
     halo_send,
@@ -169,41 +170,39 @@
         sources.append((to_chip(k, z, x, from_core), mine))
 
     barrier = pltpu.get_barrier_semaphore()
-
-    def hail(target):
+    east = (lat, lax.rem(lon + 1, LONS))
+    west = (lat, lax.rem(lon + LONS - 1, LONS))
+    north = (lax.rem(lat + LATS - 1, LATS), lon)
+    south = (lax.rem(lat + 1, LATS), lon)
+    near = [east, west, north, south, pair_peer] + [back for _, _, back in x_peers]
+    for step in (1, 2, 6, 7):
+        near.append(to_chip(y, lax.rem(z + step, 8), x, core))
+        near += [to_chip(lax.rem(y + step, 8), z, x, c) for c in (core, other)]
+    for target in near:
         pl.semaphore_signal(barrier, inc=1, device_id=target, device_id_type=MESH)
-
-    for _, _, target in around:
-        hail(target)
-    hail(pair_peer)
-    for _, _, back in x_peers + z_peers:
-        hail(back)
-    for target, mine in sources:
-
-        @pl.when(jnp.logical_not(mine))
-        def _():
-            hail(target)
-
-    expected = 8 + 1 + 3 + 7 + 8 - jnp.where(core == from_core, 1, 0)
-    pl.semaphore_wait(barrier, expected)
-
-    halo_copies = []
-    for idx, (row_step, col_step, target) in enumerate(around):
-        if row_step == -1:
-            src, dst_rows = tokens_hbm.at[pl.ds(0, 1)], pl.ds(ROWS + 1, 1)
-        elif row_step == 1:
-            src, dst_rows = tokens_hbm.at[pl.ds(ROWS - 1, 1)], pl.ds(0, 1)
-        else:
-            src, dst_rows = tokens_hbm, pl.ds(1, ROWS)
-        copy = remote(
-            src,
-            frame.at[dst_rows, pl.ds((1 - col_step) * COLS, COLS)],
-            halo_send.at[idx],
-            halo_recv.at[idx],
-            target,
-        )
+    pl.semaphore_wait(barrier, len(near))
+
+    def halo_copy(idx, src, rows, cols, target):
+        dst = frame.at[rows, cols]
+        copy = remote(src, dst, halo_send.at[idx], halo_recv.at[idx], target)
         copy.start()
-        halo_copies.append(copy)
+        return copy
+
+    left, centre, right = (pl.ds(COLS * part, COLS) for part in range(3))
+    first, last = pl.ds(0, 1), pl.ds(ROWS - 1, 1)
+    above_row, below_row = pl.ds(0, 1), pl.ds(ROWS + 1, 1)
+    halo_copies = [
+        halo_copy(0, tokens_hbm, pl.ds(1, ROWS), left, east),
+        halo_copy(1, tokens_hbm, pl.ds(1, ROWS), right, west),
+        halo_copy(2, tokens_hbm.at[first], below_row, centre, north),
+        halo_copy(3, tokens_hbm.at[last], above_row, centre, south),
+    ]
+    for step in (2, 6):
+        for target in (
+            to_chip(y, lax.rem(z + step, 8), x, core),
+            to_chip(lax.rem(y + step, 8), z, x, core),
+        ):
+            pl.semaphore_signal(far_sem, inc=1, device_id=target, device_id_type=MESH)
 
     def ones_where(equal):
         return jnp.where(equal, 1.0, 0.0).astype(BF16)
@@ -267,15 +266,15 @@
     turned_own[...] = nt(perm_x[...], x_own).astype(BF16)
     canvas[...] = jnp.zeros_like(canvas)
 
-    sides = [idx for idx, (row_step, _, _) in enumerate(around) if row_step == 0]
-    for idx in sides:
+    for idx, cols in ((0, left), (1, right)):
         halo_copies[idx].wait()
+        halo_copies.append(halo_copy(4 + idx, frame.at[pl.ds(1, 1), cols], below_row, cols, north))
+        halo_copies.append(halo_copy(6 + idx, frame.at[pl.ds(ROWS, 1), cols], above_row, cols, south))
     middle = frame[1 : ROWS + 1].reshape(ROWS * SPAN, C)
     kv_ref[SPAN : SPAN + ROWS * SPAN] = nn(middle, w_qkv[:, C:]).astype(BF16)
     turned_mid[...] = nt(perm_x[...], middle).astype(BF16)
-    for idx, copy in enumerate(halo_copies):
-        if idx not in sides:
-            copy.wait()
+    for copy in halo_copies[2:]:
+        copy.wait()
 
     @pl.when(lat == 0)
     def _():
@@ -514,6 +513,7 @@
         at = (r + 1) * SPAN + COLS
         own_ref[r] = canvas[at : at + COLS, :C] + query_part[r * COLS : (r + 1) * COLS]
 
+    pl.semaphore_wait(far_sem, 4)
     send_z(1)
     mixed = nn(mix_in[:, :C], w_out[...]) + nn(mix_in[:, C:], w_disco[...])
     mixed_ref[...] = mixed.astype(BF16).reshape(ROWS, COLS, C)
@@ -609,6 +609,7 @@
             VMEM((2, 64, 128), BF16),
             VMEM((2, ROWS, COLS, C), BF16),
             VMEM((6, COLS, C), BF16),
+            pltpu.SemaphoreType.REGULAR,
             dma((5,)),
             dma((2,)),
             dma((8,)),

time: 56.6 us -> 55.9 us (0.988)
  Pallas kernels: 55.8 us -> 55.1 us
    pallas_call x1, Pallas kernels: 54.2 us -> 53.5 us  [whole(): pl.pallas_call(whole_kernel, out_shape=(jax.ShapeDtypeStruct((ROWS, COLS,...]
where the time goes in v4:
time: 55.9 us; the launch traced here: 55.7 us
  Pallas kernels  55.1 us (99%)
  between operations  0.64 us (1%)
    pallas_call x1, Pallas kernels, whole(): pl.pallas_call(whole_kernel, out_shape=(jax.ShapeDtypeStruct((ROWS, COLS,...  53.5 us
    pallas_call x1, Pallas kernels, finish(): pl.pallas_call(finish_kernel, out_shape=(jax.ShapeDtypeStruct((ROWS, COLS...  1.64 us

profile of v4, /device:TPU:1, one launch (start us, length us, event | category | flops | bytes accessed | tf_op | source)
XLA Modules:
  0.0 55.7 jit_solution(16662092721625578535)
XLA Ops:
  0.6 53.5 %shard_map.103 = (bf16[4,32,384]{2,1,0:T(8,128)(2,1)}, bf16[4,32,384]{2,1,0:T(8,128)(2,1)}, bf16[8,32,128]{2,1,0:T(8,128)(2,1)}) custom-call(bf16[4,32,384]{2,1,0:T(8,128)(2,1)} %tokens_hbm.1, bf16[4,32,384]{2,1,0:T(8,128)(2,1)} %cot_hbm.1, bf16[384,1152]{1,0:T(8,128)(2,1)} %w_qkv_hbm.1, bf16[384,384]{1,0:T(8,128)(2,1)} %w_out_hbm.1, ...), custom_call_target="tpu_custom_call" | custom-call | tf_op jit(solution)/shard_map/pallas_call | solution.py:568
  54.1 1.6 %shard_map.104 = (bf16[4,32,384]{2,1,0:T(8,128)(2,1)}, bf16[4,32,384]{2,1,0:T(8,128)(2,1)}, f32[1728]{0:T(1024)}) custom-call(bf16[4,32,384]{2,1,0:T(8,128)(2,1)} %get-tuple-element.6.mixed_in, bf16[4,32,384]{2,1,0:T(8,128)(2,1)} %get-tuple-element.7.input_in, bf16[8,32,128]{2,1,0:T(8,128)(2,1)} %get-tuple-element.8.lines_ref), custom_call_target="tpu_custom_call" | custom-call | tf_op jit(solution)/shard_map/pallas_call | solution.py:661

commit v5 on v4

--- a/solution.py
+++ b/solution.py
@@ -84,7 +84,9 @@
     mixed_ref,
     input_ref,
     frame,
-    cot_ref,
+    cots,
+    slices,
+    slices_in,
     w_qkv,
     w_out,
     w_disco,
@@ -118,6 +120,12 @@
     far_sem,
     load_sem,
     store_sem,
+    cot_send,
+    cot_recv,
+    swap_send,
+    swap_recv,
+    slice_send,
+    slice_recv,
     halo_send,
     halo_recv,
     pair_send,
@@ -135,11 +143,12 @@
     y, x, core = lat // 4, lon // 4, lax.rem(lon, 2)
     z = lax.rem(lat, 4) * 2 + lax.rem(lon, 4) // 2
     other = 1 - core
+    slot = core * 4 + x
 
     loads = [
         pltpu.make_async_copy(tokens_hbm, frame.at[pl.ds(1, ROWS), pl.ds(COLS, COLS)], load_sem.at[0]),
         pltpu.make_async_copy(w_qkv_hbm, w_qkv, load_sem.at[1]),
-        pltpu.make_async_copy(cot_hbm, cot_ref, load_sem.at[2]),
+        pltpu.make_async_copy(cot_hbm, cots.at[slot], load_sem.at[2]),
         pltpu.make_async_copy(w_out_hbm, w_out, load_sem.at[3]),
         pltpu.make_async_copy(w_disco_hbm, w_disco, load_sem.at[4]),
     ]
@@ -174,7 +183,9 @@
     west = (lat, lax.rem(lon + LONS - 1, LONS))
     north = (lax.rem(lat + LATS - 1, LATS), lon)
     south = (lax.rem(lat + 1, LATS), lon)
-    near = [east, west, north, south, pair_peer] + [back for _, _, back in x_peers]
+    near = [east, west, north, south, pair_peer]
+    for step in (1, 2, 3):
+        near += [to_chip(y, z, lax.rem(x + step, 4), c) for c in (core, other)]
     for step in (1, 2, 6, 7):
         near.append(to_chip(y, lax.rem(z + step, 8), x, core))
         near += [to_chip(lax.rem(y + step, 8), z, x, c) for c in (core, other)]
@@ -192,10 +203,10 @@
     first, last = pl.ds(0, 1), pl.ds(ROWS - 1, 1)
     above_row, below_row = pl.ds(0, 1), pl.ds(ROWS + 1, 1)
     halo_copies = [
-        halo_copy(0, tokens_hbm, pl.ds(1, ROWS), left, east),
-        halo_copy(1, tokens_hbm, pl.ds(1, ROWS), right, west),
-        halo_copy(2, tokens_hbm.at[first], below_row, centre, north),
-        halo_copy(3, tokens_hbm.at[last], above_row, centre, south),
+        halo_copy(0, tokens_hbm.at[first], below_row, centre, north),
+        halo_copy(1, tokens_hbm.at[last], above_row, centre, south),
+        halo_copy(2, tokens_hbm, pl.ds(1, ROWS), left, east),
+        halo_copy(3, tokens_hbm, pl.ds(1, ROWS), right, west),
     ]
     for step in (2, 6):
         for target in (
@@ -203,6 +214,12 @@
             to_chip(lax.rem(y + step, 8), z, x, core),
         ):
             pl.semaphore_signal(far_sem, inc=1, device_id=target, device_id_type=MESH)
+
+    cot_copies = []
+    for d, (_, target, _) in enumerate(x_peers):
+        copy = remote(cot_hbm, cots.at[slot], cot_send.at[d], cot_recv.at[d], target)
+        copy.start()
+        cot_copies.append(copy)
 
     def ones_where(equal):
         return jnp.where(equal, 1.0, 0.0).astype(BF16)
@@ -259,21 +276,23 @@
     for load in loads:
         load.wait()
     x_own = frame[1 : ROWS + 1, COLS : 2 * COLS].reshape(CELLS, C)
-    cot = cot_ref[...].reshape(CELLS, C)
+    cot = cots[slot].reshape(CELLS, C)
     queries = nn(x_own, w_qkv[:, :C]).astype(BF16)
     upstream = nt(cot, w_out[...]).astype(BF16)
+    for idx, row in ((0, below_row), (1, above_row)):
+        halo_copies[idx].wait()
+        halo_copies.append(halo_copy(4 + idx, frame.at[row, centre], row, left, east))
+        halo_copies.append(halo_copy(6 + idx, frame.at[row, centre], row, right, west))
     gs_ref[...] = nt(cot, w_disco[...]).astype(BF16).astype(F32)
     turned_own[...] = nt(perm_x[...], x_own).astype(BF16)
     canvas[...] = jnp.zeros_like(canvas)
 
-    for idx, cols in ((0, left), (1, right)):
-        halo_copies[idx].wait()
-        halo_copies.append(halo_copy(4 + idx, frame.at[pl.ds(1, 1), cols], below_row, cols, north))
-        halo_copies.append(halo_copy(6 + idx, frame.at[pl.ds(ROWS, 1), cols], above_row, cols, south))
+    for copy in halo_copies[2:4]:
+        copy.wait()
     middle = frame[1 : ROWS + 1].reshape(ROWS * SPAN, C)
     kv_ref[SPAN : SPAN + ROWS * SPAN] = nn(middle, w_qkv[:, C:]).astype(BF16)
     turned_mid[...] = nt(perm_x[...], middle).astype(BF16)
-    for copy in halo_copies[2:]:
+    for copy in halo_copies[4:]:
         copy.wait()
 
     @pl.when(lat == 0)
@@ -341,10 +360,34 @@
     for r in range(ROWS):
         mix_in[r * COLS : (r + 1) * COLS, :C] = fold_heads(low_ref[r], C, key_rows(r)).astype(BF16)
 
-    def mix_weights(half):
-        window = mix_in[:, pl.ds(pl.multiple_of(512 * half, 128), 640)]
+    for half in range(2):
+        window = mix_in[:, 512 * half : 512 * half + 640]
         turned = nt(perm_od[half], window).astype(BF16)
-        grads[1, pl.ds(4 * half, 4)] = nn(turned, cot).astype(BF16).reshape(4, CHUNK, C)
+        slices[4 * half : 4 * half + 4] = turned.reshape(4, CHUNK, CELLS)
+    slice_copies = []
+    for d in (2, 1, 3, 0):
+        for c in range(2):
+            if d or c:
+                there = lax.rem(x + d, 4)
+                to_core = other if c else core
+                copy = remote(
+                    slices.at[to_core * 4 + there],
+                    slices_in.at[slot],
+                    slice_send.at[2 * d + c],
+                    slice_recv.at[2 * d + c],
+                    to_chip(y, z, there, to_core),
+                )
+                copy.start()
+                slice_copies.append(copy)
+    slices_in[slot] = slices[slot]
+    swaps = []
+    for copy in cot_copies:
+        copy.wait()
+    for step in range(4):
+        held = core * 4 + lax.rem(x + step, 4)
+        copy = remote(cots.at[held], cots.at[held], swap_send.at[step], swap_recv.at[step], pair_peer)
+        copy.start()
+        swaps.append(copy)
 
     def pair_copy(job, step):
         there = lax.rem(x + step, 4)
@@ -395,11 +438,17 @@
             x_copy(job, d).start()
 
     def send_z(job):
-        pair_copy(job, 0).wait()
-        total = grads[job, core * 4 + x].astype(F32) + pair_in[job, x].astype(F32)
-        for d in range(3):
-            x_copy(job, d).wait()
-            total = total + x_in[job, d].astype(F32)
+        if job == 1:
+            for copy in swaps + slice_copies:
+                copy.wait()
+            whole_slice = jnp.concatenate([slices_in[k] for k in range(8)], axis=1)
+            total = nn(whole_slice, cots[...].reshape(8 * CELLS, C))
+        else:
+            pair_copy(job, 0).wait()
+            total = grads[job, slot].astype(F32) + pair_in[job, x].astype(F32)
+            for d in range(3):
+                x_copy(job, d).wait()
+                total = total + x_in[job, d].astype(F32)
         total_ref[job, 0:8] = jnp.zeros((8, C), F32)
         total_ref[job, 8 : 8 + CHUNK] = total
         total_ref[job, 8 + CHUNK : 32 + CHUNK] = jnp.zeros((24, C), F32)
@@ -440,16 +489,11 @@
                 def _():
                     last_in[y] = last_out[job, half * 32 : half * 32 + 32]
 
-    mix_weights(other)
-    send_pair(1)
-    mix_weights(core)
-
     for r in range(ROWS):
         grad_prob = nt(kv_ref[key_rows(r), C:], u_heads[r]).astype(BF16).astype(F32)
         probs = probs_ref[r]
         mean = jnp.sum(probs * grad_prob, axis=0, keepdims=True)
         glow_ref[r] = (probs * (grad_prob - mean)).astype(BF16)
-    send_x(1)
     for r in range(ROWS):
         cells = slice(r * COLS, (r + 1) * COLS)
         dq_ref[cells] = (fold_heads(glow_ref[r], 0, key_rows(r)) * SCALING).astype(BF16)
@@ -578,7 +622,9 @@
             VMEM((ROWS, COLS, C), BF16),
             VMEM((ROWS, COLS, C), BF16),
             VMEM((ROWS + 2, SPAN, C), BF16),
-            VMEM((ROWS, COLS, C), BF16),
+            VMEM((8, ROWS, COLS, C), BF16),
+            VMEM((8, CHUNK, CELLS), BF16),
+            VMEM((8, CHUNK, CELLS), BF16),
             VMEM((C, 3 * C), BF16),
             VMEM((C, C), BF16),
             VMEM((2 * C, C), BF16),
@@ -596,12 +642,12 @@
             VMEM((CELLS, 3 * C), BF16),
             VMEM((CELLS, C), BF16),
             VMEM((CELLS, 2 * C), F32),
-            VMEM((2, 8, CHUNK, C), BF16),
+            VMEM((1, 8, CHUNK, C), BF16),
             VMEM((ROWS, COLS, C), F32),
             VMEM((ROWS + 2, SPAN, C), BF16),
-            VMEM((2, 4, CHUNK, C), BF16),
-            VMEM((2, 3, CHUNK, C), BF16),
-            VMEM((2, 3, CHUNK, C), BF16),
+            VMEM((1, 4, CHUNK, C), BF16),
+            VMEM((1, 3, CHUNK, C), BF16),
+            VMEM((1, 3, CHUNK, C), BF16),
             VMEM((2, CHUNK + 32, C), F32),
             VMEM((2, 8 * 64 + 16, 128), F32),
             VMEM((2, 8, 64, 128), BF16),
@@ -612,12 +658,18 @@
             pltpu.SemaphoreType.REGULAR,
             dma((5,)),
             dma((2,)),
+            dma((3,)),
+            dma((3,)),
+            dma((4,)),
+            dma((4,)),
             dma((8,)),
             dma((8,)),
-            dma((2, 4)),
-            dma((2, 4)),
-            dma((2, 3)),
-            dma((2, 3)),
+            dma((8,)),
+            dma((8,)),
+            dma((1, 4)),
+            dma((1, 4)),
+            dma((1, 3)),
+            dma((1, 3)),
             dma((2, 7)),
             dma((2, 7)),
             dma((2, 4)),

time: 55.9 us -> 51.4 us (0.919)
  Pallas kernels: 55.1 us -> 50.6 us
    pallas_call x1, Pallas kernels: 53.5 us -> 48.9 us  [whole(): pl.pallas_call(whole_kernel, out_shape=(jax.ShapeDtypeStruct((ROWS, COLS,...]
where the time goes in v5:
time: 51.4 us; the launch traced here: 51.2 us
  Pallas kernels  50.6 us (98%)
  between operations  0.64 us (1%)
    pallas_call x1, Pallas kernels, whole(): pl.pallas_call(whole_kernel, out_shape=(jax.ShapeDtypeStruct((ROWS, COLS,...  48.9 us
    pallas_call x1, Pallas kernels, finish(): pl.pallas_call(finish_kernel, out_shape=(jax.ShapeDtypeStruct((ROWS, COLS...  1.64 us

profile of v5, /device:TPU:1, one launch (start us, length us, event | category | flops | bytes accessed | tf_op | source)
XLA Modules:
  0.0 51.2 jit_solution(2304157588236168916)
XLA Ops:
  0.6 48.9 %shard_map.103 = (bf16[4,32,384]{2,1,0:T(8,128)(2,1)}, bf16[4,32,384]{2,1,0:T(8,128)(2,1)}, bf16[8,32,128]{2,1,0:T(8,128)(2,1)}) custom-call(bf16[4,32,384]{2,1,0:T(8,128)(2,1)} %tokens_hbm.1, bf16[4,32,384]{2,1,0:T(8,128)(2,1)} %cot_hbm.1, bf16[384,1152]{1,0:T(8,128)(2,1)} %w_qkv_hbm.1, bf16[384,384]{1,0:T(8,128)(2,1)} %w_out_hbm.1, ...), custom_call_target="tpu_custom_call" | custom-call | tf_op jit(solution)/shard_map/pallas_call | solution.py:612
  49.6 1.6 %shard_map.104 = (bf16[4,32,384]{2,1,0:T(8,128)(2,1)}, bf16[4,32,384]{2,1,0:T(8,128)(2,1)}, f32[1728]{0:T(1024)}) custom-call(bf16[4,32,384]{2,1,0:T(8,128)(2,1)} %get-tuple-element.6.mixed_in, bf16[4,32,384]{2,1,0:T(8,128)(2,1)} %get-tuple-element.7.input_in, bf16[8,32,128]{2,1,0:T(8,128)(2,1)} %get-tuple-element.8.lines_ref), custom_call_target="tpu_custom_call" | custom-call | tf_op jit(solution)/shard_map/pallas_call | solution.py:713

commit v6 on v5

--- a/solution.py
+++ b/solution.py
@@ -183,7 +183,7 @@
     west = (lat, lax.rem(lon + LONS - 1, LONS))
     north = (lax.rem(lat + LATS - 1, LATS), lon)
     south = (lax.rem(lat + 1, LATS), lon)
-    near = [east, west, north, south, pair_peer]
+    near = [north, south, east, west, pair_peer]
     for step in (1, 2, 3):
         near += [to_chip(y, z, lax.rem(x + step, 4), c) for c in (core, other)]
     for step in (1, 2, 6, 7):
@@ -285,7 +285,6 @@
         halo_copies.append(halo_copy(6 + idx, frame.at[row, centre], row, right, west))
     gs_ref[...] = nt(cot, w_disco[...]).astype(BF16).astype(F32)
     turned_own[...] = nt(perm_x[...], x_own).astype(BF16)
-    canvas[...] = jnp.zeros_like(canvas)
 
     for copy in halo_copies[2:4]:
         copy.wait()
@@ -446,7 +445,7 @@
         else:
             pair_copy(job, 0).wait()
             total = grads[job, slot].astype(F32) + pair_in[job, x].astype(F32)
-            for d in range(3):
+            for d in (0, 2, 1):
                 x_copy(job, d).wait()
                 total = total + x_in[job, d].astype(F32)
         total_ref[job, 0:8] = jnp.zeros((8, C), F32)
@@ -497,11 +496,16 @@
     for r in range(ROWS):
         cells = slice(r * COLS, (r + 1) * COLS)
         dq_ref[cells] = (fold_heads(glow_ref[r], 0, key_rows(r)) * SCALING).astype(BF16)
-        canvas[key_rows(r), :C] += nn(glow_ref[r], q_heads[r]) * SCALING
-        canvas[key_rows(r), C:] += nn(low_ref[r], u_heads[r])
+        both = jnp.concatenate([nn(glow_ref[r], q_heads[r]), nn(low_ref[r], u_heads[r])], axis=1)
+        if r == 0:
+            canvas[key_rows(0)] = both
+        else:
+            begun = slice(r * SPAN, (r + 2) * SPAN)
+            canvas[begun] += both[: 2 * SPAN]
+            canvas[(r + 2) * SPAN : (r + 3) * SPAN] = both[2 * SPAN :]
 
     grad_query = dq_ref[...]
-    kv_part = canvas[...].astype(BF16)
+    kv_part = jnp.concatenate([canvas[:, :C] * SCALING, canvas[:, C:]], axis=1).astype(BF16)
     kv_middle = kv_part[SPAN : SPAN + ROWS * SPAN]
     kv_edges = jnp.concatenate([kv_part[:SPAN], kv_part[FRAME - SPAN :]], axis=0)
     turned_edge[...] = nt(perm_x[...], edges).astype(BF16)
@@ -551,7 +555,8 @@
             src = rim_ref.at[row, pl.ds((1 + col_step) * COLS, COLS)]
             dst = line_in.at[(0 if row_step == -1 else 3) + col_step + 1]
         copy = remote(src, dst, rim_send.at[idx], rim_recv.at[idx], target)
-        copy.start()
+        if row_step:
+            copy.start()
         rim_copies.append(copy)
     for r in range(ROWS):
         at = (r + 1) * SPAN + COLS
@@ -564,7 +569,12 @@
     mixed_store = pltpu.make_async_copy(mixed_ref, mixed_hbm, store_sem.at[0])
     mixed_store.start()
     send_z(0)
+    for idx, (row_step, _, _) in enumerate(around):
+        if row_step == 0:
+            rim_copies[idx].start()
     send_last(1)
+
+    send_last(0)
 
     for copy in rim_copies:
         copy.wait()
@@ -581,7 +591,6 @@
     input_store = pltpu.make_async_copy(input_ref, input_hbm, store_sem.at[1])
     input_store.start()
 
-    send_last(0)
     for k, (source, mine) in enumerate(sources):
 
         @pl.when(jnp.logical_not(mine))

time: 51.4 us -> 50.7 us (0.986)
  Pallas kernels: 50.6 us -> 49.9 us
    pallas_call x1, Pallas kernels: 48.9 us -> 48.3 us  [whole(): pl.pallas_call(whole_kernel, out_shape=(jax.ShapeDtypeStruct((ROWS, COLS,...]
where the time goes in v6:
time: 50.7 us; the launch traced here: 50.5 us
  Pallas kernels  49.9 us (98%)
  between operations  0.64 us (1%)
    pallas_call x1, Pallas kernels, whole(): pl.pallas_call(whole_kernel, out_shape=(jax.ShapeDtypeStruct((ROWS, COLS,...  48.3 us
    pallas_call x1, Pallas kernels, finish(): pl.pallas_call(finish_kernel, out_shape=(jax.ShapeDtypeStruct((ROWS, COLS...  1.64 us

profile of v6, /device:TPU:1, one launch (start us, length us, event | category | flops | bytes accessed | tf_op | source)
XLA Modules:
  0.0 50.5 jit_solution(4740010518536984611)
XLA Ops:
  0.6 48.3 %shard_map.103 = (bf16[4,32,384]{2,1,0:T(8,128)(2,1)}, bf16[4,32,384]{2,1,0:T(8,128)(2,1)}, bf16[8,32,128]{2,1,0:T(8,128)(2,1)}) custom-call(bf16[4,32,384]{2,1,0:T(8,128)(2,1)} %tokens_hbm.1, bf16[4,32,384]{2,1,0:T(8,128)(2,1)} %cot_hbm.1, bf16[384,1152]{1,0:T(8,128)(2,1)} %w_qkv_hbm.1, bf16[384,384]{1,0:T(8,128)(2,1)} %w_out_hbm.1, ...), custom_call_target="tpu_custom_call" | custom-call | tf_op jit(solution)/shard_map/pallas_call | solution.py:621
  48.9 1.6 %shard_map.104 = (bf16[4,32,384]{2,1,0:T(8,128)(2,1)}, bf16[4,32,384]{2,1,0:T(8,128)(2,1)}, f32[1728]{0:T(1024)}) custom-call(bf16[4,32,384]{2,1,0:T(8,128)(2,1)} %get-tuple-element.6.mixed_in, bf16[4,32,384]{2,1,0:T(8,128)(2,1)} %get-tuple-element.7.input_in, bf16[8,32,128]{2,1,0:T(8,128)(2,1)} %get-tuple-element.8.lines_ref), custom_call_target="tpu_custom_call" | custom-call | tf_op jit(solution)/shard_map/pallas_call | solution.py:722

commit v7 on v6

--- a/solution.py
+++ b/solution.py
@@ -205,6 +205,13 @@
     halo_copies = [
         halo_copy(0, tokens_hbm.at[first], below_row, centre, north),
         halo_copy(1, tokens_hbm.at[last], above_row, centre, south),
+    ]
+    cot_copies = []
+    for d, (_, target, _) in enumerate(x_peers):
+        copy = remote(cot_hbm, cots.at[slot], cot_send.at[d], cot_recv.at[d], target)
+        copy.start()
+        cot_copies.append(copy)
+    halo_copies += [
         halo_copy(2, tokens_hbm, pl.ds(1, ROWS), left, east),
         halo_copy(3, tokens_hbm, pl.ds(1, ROWS), right, west),
     ]
@@ -214,12 +221,6 @@
             to_chip(lax.rem(y + step, 8), z, x, core),
         ):
             pl.semaphore_signal(far_sem, inc=1, device_id=target, device_id_type=MESH)
-
-    cot_copies = []
-    for d, (_, target, _) in enumerate(x_peers):
-        copy = remote(cot_hbm, cots.at[slot], cot_send.at[d], cot_recv.at[d], target)
-        copy.start()
-        cot_copies.append(copy)
 
     def ones_where(equal):
         return jnp.where(equal, 1.0, 0.0).astype(BF16)
@@ -525,8 +526,8 @@
     send_pair(0)
     token_weights(core)
 
+    send_x(0)
     canvas[:, :C] = nt(kv_part, w_qkv[:, C:])
-    send_x(0)
     query_part = nt(grad_query, w_qkv[:, :C])
     margin = jnp.zeros((16, C), F32)
     for row in range(ROWS + 2):

time: 50.7 us -> 50.7 us (level)
  no operation moved by 1% of the time
where the time goes in v7:
time: 50.7 us; the launch traced here: 50.6 us
  Pallas kernels  49.9 us (98%)
  between operations  0.64 us (1%)
    pallas_call x1, Pallas kernels, whole(): pl.pallas_call(whole_kernel, out_shape=(jax.ShapeDtypeStruct((ROWS, COLS,...  48.3 us
    pallas_call x1, Pallas kernels, finish(): pl.pallas_call(finish_kernel, out_shape=(jax.ShapeDtypeStruct((ROWS, COLS...  1.64 us

profile of v7, /device:TPU:1, one launch (start us, length us, event | category | flops | bytes accessed | tf_op | source)
XLA Modules:
  0.0 50.6 jit_solution(10481473107975678829)
XLA Ops:
  0.6 48.3 %shard_map.103 = (bf16[4,32,384]{2,1,0:T(8,128)(2,1)}, bf16[4,32,384]{2,1,0:T(8,128)(2,1)}, bf16[8,32,128]{2,1,0:T(8,128)(2,1)}) custom-call(bf16[4,32,384]{2,1,0:T(8,128)(2,1)} %tokens_hbm.1, bf16[4,32,384]{2,1,0:T(8,128)(2,1)} %cot_hbm.1, bf16[384,1152]{1,0:T(8,128)(2,1)} %w_qkv_hbm.1, bf16[384,384]{1,0:T(8,128)(2,1)} %w_out_hbm.1, ...), custom_call_target="tpu_custom_call" | custom-call | tf_op jit(solution)/shard_map/pallas_call | solution.py:622
  48.9 1.6 %shard_map.104 = (bf16[4,32,384]{2,1,0:T(8,128)(2,1)}, bf16[4,32,384]{2,1,0:T(8,128)(2,1)}, f32[1728]{0:T(1024)}) custom-call(bf16[4,32,384]{2,1,0:T(8,128)(2,1)} %get-tuple-element.6.mixed_in, bf16[4,32,384]{2,1,0:T(8,128)(2,1)} %get-tuple-element.7.input_in, bf16[8,32,128]{2,1,0:T(8,128)(2,1)} %get-tuple-element.8.lines_ref), custom_call_target="tpu_custom_call" | custom-call | tf_op jit(solution)/shard_map/pallas_call | solution.py:723
